TPU v7x, 32 devices: a whole 2x2x4 slice. The times are simulated.
32 devices in a mesh: px: 8 (over z, x), py: 4 (over y, core).
Axes of the slice: x: 2, y: 2, z: 4, core: 2. Of those that a mesh axis runs over, the one named last changes fastest.
Arguments:
- start_field: float32 [512, 512, 256], P('px', 'py'), may hold values from 0.25 to 4
- end_adjoint: float32 [512, 512, 256], P('px', 'py'), may hold values from 0.25 to 4
- potential: float32 [512, 512, 256], P('px', 'py'), may hold values from -15 to 15
- line_xy: float32 [512, 512], replicated, may hold values from -1 to 2
- line_z: float32 [256, 256], replicated, may hold values from -1 to 2
Outputs:
- final_field: float32 [512, 512, 256], P('px', 'py')
- first_adjoint: float32 [512, 512, 256], P('px', 'py')
- density: float32 [512, 512, 256], P('px', 'py')
All inputs are finite; a program needn't handle non-finite values.
Results may differ from a plain program's by a relative error of at most 0.0001.
Values sent between devices are 32-bit elements; how exact they have to be, the bound alone decides.
No kernel may reach another device: no remote copies, remote signals or barrier semaphores. Data moves between devices by JAX's collectives and lax.ppermute only.
A program may use at most 256 MiB of HBM per device.

v0:
```python
import jax
import jax.numpy as jnp
from jax import lax
from jax.sharding import PartitionSpec as P

STEPS = 1


def product(left, right):
    return jnp.dot(left, right, precision=lax.Precision.HIGHEST, preferred_element_type=jnp.float32)


def body(start_field, end_adjoint, potential, line_xy, line_z):
    count_px = lax.axis_size("px")
    count_py = lax.axis_size("py")
    cells_x, cells_y, full_z = start_field.shape
    full_x = line_xy.shape[0]
    block_z = full_z // count_py
    block_y = full_x // count_px
    xy_turned = line_xy.T
    z_turned = line_z.T

    def sweep_last(stacked, kinds):
        pieces = [product(stacked[0], line_z if kinds[0] else z_turned)]
        return jnp.stack(pieces)

    def sweep_first(stacked, kinds):
        pieces = [product(xy_turned if kinds[0] else line_xy, stacked[0])]
        return jnp.stack(pieces)

    def z_to_y(stacked):
        fields = stacked.shape[0]
        send = stacked.reshape(fields, cells_x, cells_y, count_py, block_z).transpose(0, 2, 3, 1, 4)
        send = send.reshape(fields, cells_y, count_py * cells_x * block_z)
        return lax.all_to_all(send, "py", split_axis=2, concat_axis=1, tiled=True)

    def y_to_x(stacked):
        fields = stacked.shape[0]
        send = stacked.reshape(fields, full_x, cells_x, block_z).transpose(0, 2, 1, 3)
        send = send.reshape(fields, cells_x, full_x * block_z)
        return lax.all_to_all(send, "px", split_axis=2, concat_axis=1, tiled=True)

    def x_to_y(stacked):
        fields = stacked.shape[0]
        send = stacked.reshape(fields, full_x, block_y, block_z).transpose(0, 2, 1, 3)
        send = send.reshape(fields, block_y, full_x * block_z)
        return lax.all_to_all(send, "px", split_axis=2, concat_axis=1, tiled=True)

    def y_to_z(stacked):
        fields = stacked.shape[0]
        send = stacked.reshape(fields, count_py, cells_y, cells_x, block_z)
        got = lax.all_to_all(send, "py", split_axis=1, concat_axis=4, tiled=True)
        got = got.reshape(fields, cells_y, cells_x, count_py * block_z).transpose(0, 2, 1, 3)
        return got.reshape(fields, cells_x * cells_y, full_z)

    half_z = jnp.exp(-0.05 * potential).reshape(cells_x * cells_y, full_z)

    def contour_step(stacked, kinds):
        stacked = stacked * half_z
        stacked = sweep_last(stacked, kinds)
        stacked = z_to_y(stacked)
        stacked = sweep_first(stacked, kinds)
        stacked = y_to_x(stacked)
        stacked = sweep_first(stacked, kinds)
        stacked = y_to_z(x_to_y(stacked))
        return (stacked * half_z, "z")

    forward_list = [start_field.reshape(1, cells_x * cells_y, full_z)]
    adjoint_list = [end_adjoint.reshape(1, cells_x * cells_y, full_z)]
    layouts = ["z"]
    layout = "z"
    moved, layout = contour_step(forward_list[-1], (False,))
    forward_list.append(moved)
    layouts.append(layout)
    layout = "z"
    index = 0
    moved, layout = contour_step(adjoint_list[-1], (True,))
    adjoint_list.append(moved)
    adjoint_list = adjoint_list[::-1]
    density_z = jnp.zeros((cells_x * cells_y, full_z), jnp.float32)
    for index in range(STEPS + 1):
        weight = 0.5
        term = 0.1 * weight * forward_list[index][0] * adjoint_list[index][0]
        density_z = density_z + term
    shape = (cells_x, cells_y, full_z)
    return (
        forward_list[-1][0].reshape(shape),
        adjoint_list[0][0].reshape(shape),
        density_z.reshape(shape),
    )


def solution(mesh):
    placed = (P("px", "py", None), P("px", "py", None), P("px", "py", None), P(), P())
    return jax.shard_map(
        body,
        mesh=mesh,
        in_specs=placed,
        out_specs=(P("px", "py", None), P("px", "py", None), P("px", "py", None)),
        check_vma=False,
    )
```

profile of v0, /device:TPU:12, one launch (start us, length us, event | category | flops | bytes accessed | tf_op | source)
XLA Modules:
  0.0 1676.8 jit_solution(2524713279621208677)
XLA Ops:
  70.2 65.1 %all-to-all-done.4 = f32[1,128,16384]{1,0,2:T(1,128)} async-done(((f32[1,128,16384]{1,0,2:T(1,128)}), f32[1,128,16384]{1,0,2:T(1,128)}, u32[]{:S(2)}, u32[]{:S(2)}) %all-to-all-start.4) | async-done | bytes 8388640 | tf_op jit(solution)/shard_map/all_to_all | solution.py:35
  151.7 16.8 %fusion.22 = f32[4096,512]{1,0:T(8,128)} fusion(f32[512,4096]{1,0:T(8,128)} %bitcast.130, f32[512,512]{1,0:T(8,128)S(1)} %copy-done), kind=kOutput, calls=%fused_computation.18 | convolution fusion | flops 12884901888 | bytes 17825792 | tf_op jit(solution)/shard_map/dot_general | solution.py:10
  180.8 18.1 %copy.107 = f32[1,64,512,64]{1,3,2,0:T(8,128)} copy(f32[1,64,512,64]{3,2,1,0:T(8,128)} %bitcast.119) | data formatting | bytes 16777216 | tf_op jit(solution)/shard_map/reshape | solution.py:40
  199.4 146.4 %reduce = f32[32768,64]{1,0:T(8,128)} reduce(f32[32768,1,64]{2,1,0:T(1,128)} %bitcast.118, f32[]{:T(128)} %broadcast.7), dimensions={1}, to_apply=%bitcast.100.reduce_sub_computation | reduce | bytes 16777220
  376.9 29.6 %fusion.20 = f32[4096,512]{1,0:T(8,128)} fusion(f32[512,4096]{1,0:T(8,128)} %bitcast.131, f32[512,512]{1,0:T(8,128)S(1)} %copy-done), kind=kOutput, calls=%fused_computation.16 | convolution fusion | flops 12884901888 | bytes 17825792 | tf_op jit(solution)/shard_map/dot_general | solution.py:10
  418.8 18.1 %copy.102 = f32[1,64,512,64]{1,3,2,0:T(8,128)} copy(f32[1,64,512,64]{3,2,1,0:T(8,128)} %bitcast.120) | data formatting | bytes 16777216 | tf_op jit(solution)/shard_map/reshape | solution.py:40
  436.9 146.4 %reduce.4 = f32[32768,64]{1,0:T(8,128)} reduce(f32[32768,1,64]{2,1,0:T(1,128)} %bitcast.121, f32[]{:T(128)} %broadcast.7), dimensions={1}, to_apply=%bitcast.96.reduce_sub_computation | reduce | bytes 16777220
  604.8 26.3 %reduce.1 = f32[8,262144]{1,0:T(8,128)} reduce(f32[8,1,262144]{2,1,0:T(1,128)} %all-to-all-done.5, f32[]{:T(128)} %broadcast.7), dimensions={1}, to_apply=%all_to_all.103.reduce_sub_computation | reduce | bytes 16777220 | tf_op jit(solution)/shard_map/all_to_all | solution.py:41
  631.1 41.0 %reshape.122 = f32[32768,1,64]{2,1,0:T(1,128)} reshape(f32[8,262144]{1,0:T(8,128)} %reduce.1) | data formatting | bytes 16777216
  694.0 16.9 %fusion.23 = f32[4096,512]{1,0:T(8,128)} fusion(f32[512,4096]{1,0:T(8,128)S(1)} %bitcast.132, f32[512,512]{1,0:T(8,128)S(1)} %copy-done), kind=kOutput, calls=%fused_computation.19 | convolution fusion | flops 12884901888 | bytes 17825792 | tf_op jit(solution)/shard_map/dot_general | solution.py:10
  723.2 18.1 %copy.109 = f32[1,64,512,64]{1,3,2,0:T(8,128)} copy(f32[1,64,512,64]{3,2,1,0:T(8,128)} %bitcast.122) | data formatting | bytes 16777216 | tf_op jit(solution)/shard_map/reshape | solution.py:46
  741.3 146.6 %reduce.2 = f32[32768,64]{1,0:T(8,128)} reduce(f32[32768,1,64]{2,1,0:T(1,128)} %bitcast.123, f32[]{:T(128)} %broadcast.7), dimensions={1}, to_apply=%bitcast.102.reduce_sub_computation | reduce | bytes 16777220
  909.3 26.4 %reduce.5 = f32[8,262144]{1,0:T(8,128)} reduce(f32[8,1,262144]{2,1,0:T(1,128)} %all-to-all-done.1, f32[]{:T(128)} %broadcast.7), dimensions={1}, to_apply=%all_to_all.91.reduce_sub_computation | reduce | bytes 16777220 | tf_op jit(solution)/shard_map/all_to_all | solution.py:41
  935.7 41.3 %reshape.118 = f32[32768,1,64]{2,1,0:T(1,128)} reshape(f32[8,262144]{1,0:T(8,128)} %reduce.5) | data formatting | bytes 16777216
  998.8 30.4 %fusion.21 = f32[4096,512]{1,0:T(8,128)} fusion(f32[512,4096]{1,0:T(8,128)S(1)} %bitcast.133, f32[512,512]{1,0:T(8,128)S(1)} %copy-done), kind=kOutput, calls=%fused_computation.17 | convolution fusion | flops 12884901888 | bytes 17825792 | tf_op jit(solution)/shard_map/dot_general | solution.py:10
  1041.5 18.1 %copy.104 = f32[1,64,512,64]{1,3,2,0:T(8,128)} copy(f32[1,64,512,64]{3,2,1,0:T(8,128)} %bitcast.124) | data formatting | bytes 16777216 | tf_op jit(solution)/shard_map/reshape | solution.py:46
  1059.6 146.4 %reduce.6 = f32[32768,64]{1,0:T(8,128)} reduce(f32[32768,1,64]{2,1,0:T(1,128)} %bitcast.125, f32[]{:T(128)} %broadcast.7), dimensions={1}, to_apply=%bitcast.98.reduce_sub_computation | reduce | bytes 16777220
  1227.5 26.5 %reduce.3 = f32[8,262144]{1,0:T(8,128)} reduce(f32[8,1,262144]{2,1,0:T(1,128)} %all-to-all-done.6, f32[]{:T(128)} %broadcast.7), dimensions={1}, to_apply=%all_to_all.106.reduce_sub_computation | reduce | bytes 16777220 | tf_op jit(solution)/shard_map/all_to_all | solution.py:47
  1254.0 41.0 %reshape.124 = f32[32768,1,64]{2,1,0:T(1,128)} reshape(f32[8,262144]{1,0:T(8,128)} %reduce.3) | data formatting | bytes 16777216
  1336.4 70.3 %all-to-all-done.2 = f32[8,1,262144]{2,1,0:T(1,128)} async-done(((f32[8,1,262144]{2,1,0:T(1,128)}), f32[8,1,262144]{2,1,0:T(1,128)}, u32[]{:S(2)}, u32[]{:S(2)}) %all-to-all-start.2) | async-done | bytes 8388640 | tf_op jit(solution)/shard_map/all_to_all | solution.py:47
  1412.7 26.5 %reduce.7 = f32[8,262144]{1,0:T(8,128)} reduce(f32[8,1,262144]{2,1,0:T(1,128)} %all-to-all-done.2, f32[]{:T(128)} %broadcast.7), dimensions={1}, to_apply=%all_to_all.94.reduce_sub_computation | reduce | bytes 16777220 | tf_op jit(solution)/shard_map/all_to_all | solution.py:47
  1439.3 41.0 %reshape.120 = f32[32768,1,64]{2,1,0:T(1,128)} reshape(f32[8,262144]{1,0:T(8,128)} %reduce.7) | data formatting | bytes 16777216
  1535.8 83.3 %all-to-all-done.3 = f32[1,4,128,64,64]{2,4,3,0,1:T(8,128)} async-done(((f32[1,4,128,64,64]{2,4,3,0,1:T(8,128)}), f32[1,4,128,64,64]{2,4,3,0,1:T(8,128)}, u32[]{:S(2)}, u32[]{:S(2)}) %all-to-all-start.3) | async-done | bytes 8388640 | tf_op jit(solution)/shard_map/all_to_all | solution.py:52
  1627.5 22.1 %multiply_add_fusion = (f32[64,128,256]{1,2,0:T(8,128)}, f32[64,128,256]{1,2,0:T(8,128)}, f32[64,128,256]{1,2,0:T(8,128)}) fusion(f32[64,128,256]{1,2,0:T(8,128)} %copy.78, f32[64,128,256]{1,2,0:T(8,128)} %copy.64, f32[64,128,256]{1,2,0:T(8,128)S(1)} %bitcast.140, f32[64,128,256]{1,2,0:T(8,128)} %copy.63, f32[64,128,256]{1,2,0:T(8,128)} %bitcast.141), kind=kLoop, calls=%fused_computation.4 | loop fusion | flops 16777216 | bytes 67108864 | tf_op jit(solution)/shard_map/add | solution.py:84
  (53 shorter events, 412.7 us)
Async XLA Ops:
  0.6 151.1 %copy-start = (f32[512,512]{1,0:T(8,128)S(1)}, f32[512,512]{1,0:T(8,128)}, u32[]{:S(2)}) copy-start(f32[512,512]{1,0:T(8,128)} %param.8) | copy-start | bytes 3145732
  37.2 98.2 %all-to-all-start.4 = ((f32[1,128,16384]{1,0,2:T(1,128)}), f32[1,128,16384]{1,0,2:T(1,128)}, u32[]{:S(2)}, u32[]{:S(2)}) async-start(f32[1,128,16384]{1,0,2:T(1,128)} %bitcast.139), calls=%async_computation.4 | async-start | bytes 16777216 | tf_op jit(solution)/shard_map/all_to_all | solution.py:35
  43.8 9.0 copy-start.2
  135.3 225.9 %all-to-all-start = ((f32[1,128,16384]{1,0,2:T(1,128)}), f32[1,128,16384]{1,0,2:T(1,128)}, u32[]{:S(2)}, u32[]{:S(2)}) async-start(f32[1,128,16384]{1,0,2:T(1,128)} %bitcast.138), calls=%async_computation | async-start | bytes 16777216 | tf_op jit(solution)/shard_map/all_to_all | solution.py:35
  361.2 237.5 %all-to-all-start.5 = ((f32[8,1,262144]{2,1,0:T(1,128)}), f32[8,1,262144]{2,1,0:T(1,128)}, u32[]{:S(2)}, u32[]{:S(2)}) async-start(f32[8,1,262144]{2,1,0:T(1,128)} %reshape.121), calls=%async_computation.5 | async-start | bytes 16777216 | tf_op jit(solution)/shard_map/all_to_all | solution.py:41
  598.8 304.5 %all-to-all-start.1 = ((f32[8,1,262144]{2,1,0:T(1,128)}), f32[8,1,262144]{2,1,0:T(1,128)}, u32[]{:S(2)}, u32[]{:S(2)}) async-start(f32[8,1,262144]{2,1,0:T(1,128)} %reshape.117), calls=%async_computation.1 | async-start | bytes 16777216 | tf_op jit(solution)/shard_map/all_to_all | solution.py:41
  903.3 318.2 %all-to-all-start.6 = ((f32[8,1,262144]{2,1,0:T(1,128)}), f32[8,1,262144]{2,1,0:T(1,128)}, u32[]{:S(2)}, u32[]{:S(2)}) async-start(f32[8,1,262144]{2,1,0:T(1,128)} %reshape.123), calls=%async_computation.6 | async-start | bytes 16777216 | tf_op jit(solution)/shard_map/all_to_all | solution.py:47
  1221.5 185.2 %all-to-all-start.2 = ((f32[8,1,262144]{2,1,0:T(1,128)}), f32[8,1,262144]{2,1,0:T(1,128)}, u32[]{:S(2)}, u32[]{:S(2)}) async-start(f32[8,1,262144]{2,1,0:T(1,128)} %reshape.119), calls=%async_computation.2 | async-start | bytes 16777216 | tf_op jit(solution)/shard_map/all_to_all | solution.py:47
  1406.7 114.9 %all-to-all-start.7 = ((f32[1,4,128,64,64]{2,4,3,0,1:T(8,128)}), f32[1,4,128,64,64]{2,4,3,0,1:T(8,128)}, u32[]{:S(2)}, u32[]{:S(2)}) async-start(f32[1,4,128,64,64]{2,4,3,0,1:T(8,128)} %copy.91), calls=%async_computation.7 | async-start | bytes 16777216 | tf_op jit(solution)/shard_map/all_to_all | solution.py:52
  1521.7 97.4 %all-to-all-start.3 = ((f32[1,4,128,64,64]{2,4,3,0,1:T(8,128)}), f32[1,4,128,64,64]{2,4,3,0,1:T(8,128)}, u32[]{:S(2)}, u32[]{:S(2)}) async-start(f32[1,4,128,64,64]{2,4,3,0,1:T(8,128)} %copy.76), calls=%async_computation.3 | async-start | bytes 16777216 | tf_op jit(solution)/shard_map/all_to_all | solution.py:52
  1619.1 8.4 copy-start.1
where the time goes:
time: 1690 us; the launch traced here: 1680 us
  other arithmetic  714 us (42%)
  local copies, waits for them, and re-layouts  572 us (34%)
  waiting for transfers between devices  219 us (13%)
  matrix products  120 us (7%)
  starting transfers between devices  50.7 us (3%)
    unnamed x4, other arithmetic  586 us
    unnamed x22, local copies, waits for them, and re-layouts  282 us
    dot_general x6, matrix products, product(): jnp.dot(left, right, precision=lax.Precision.HIGHEST, preferred_element_t...  120 us
    all_to_all x2, waiting for transfers between devices, y_to_z(): got = lax.all_to_all(send, 'py', split_axis=1, concat_axis=4, tiled=True)  83.3 us
    all_to_all x2, waiting for transfers between devices, x_to_y(): return lax.all_to_all(send, 'px', split_axis=2, concat_axis=1, tiled=True)  70.3 us
    all_to_all x2, waiting for transfers between devices, z_to_y(): return lax.all_to_all(send, 'py', split_axis=2, concat_axis=1, tiled=True)  65.1 us
    reshape x4, local copies, waits for them, and re-layouts, y_to_z(): send = stacked.reshape(fields, count_py, cells_y, cells_x, block_z)  57.4 us
    all_to_all x2, other arithmetic, x_to_y(): return lax.all_to_all(send, 'px', split_axis=2, concat_axis=1, tiled=True)  53.1 us
  transfers between devices with their start and end apart: 8, of which 3 were waited for; matrix products, arithmetic and copies ran while one was open for 78% of the time, Pallas kernels for 0%

commit v1 on v0

v1 whole, which is shorter than its diff:
```python
import functools

import jax
import jax.numpy as jnp
from jax import lax
from jax.experimental import pallas as pl
from jax.experimental.pallas import tpu as pltpu
from jax.sharding import PartitionSpec as P

F32 = jnp.float32
ROWS = 8
LANES = 128
VMEM_LIMIT = 56 * 1024 * 1024


def product(left, right):
    return jnp.dot(left, right, precision=lax.Precision.HIGHEST, preferred_element_type=F32)


def two_parts(value):
    high = lax.reduce_precision(value, 8, 7)
    return [high.astype(jnp.bfloat16), (value - high).astype(jnp.bfloat16)]


def split_in_kernel(value):
    high = value.astype(jnp.bfloat16)
    return high, (value - high.astype(F32)).astype(jnp.bfloat16)


def dot(left, right):
    return jnp.dot(left, right, preferred_element_type=F32)


def lines_times(lines, matrix_refs):
    high, low = split_in_kernel(lines)
    matrix_high, matrix_low = matrix_refs[0][...], matrix_refs[1][...]
    return dot(high, matrix_high) + (dot(high, matrix_low) + dot(low, matrix_high))


def times_lines(matrix_refs, lines):
    high, low = split_in_kernel(lines)
    matrix_high, matrix_low = matrix_refs[0][...], matrix_refs[1][...]
    return dot(matrix_high, high) + (dot(matrix_low, high) + dot(matrix_high, low))


def half_of(potential):
    return jnp.exp(-0.05 * potential)


def call(kernel, name, grid, in_specs, out_specs, outs, scratch, flops, touched, aliases=None):
    return pl.pallas_call(
        kernel,
        name=name,
        grid=grid,
        in_specs=in_specs,
        out_specs=out_specs,
        out_shape=outs,
        scratch_shapes=scratch,
        input_output_aliases=aliases or {},
        cost_estimate=pl.CostEstimate(flops=flops, bytes_accessed=touched, transcendentals=0),
        compiler_params=pltpu.CompilerParams(vmem_limit_bytes=VMEM_LIMIT),
    )


def table_spec():
    return pl.BlockSpec(memory_space=pltpu.SMEM)


def whole_spec(shape):
    return pl.BlockSpec(shape, lambda i: (0,) * len(shape))


def to_of(me, r, n):
    pairs = n // 2
    return ((me // 2 + r // 2) % pairs) * 2 + (me % 2 + r % 2) % 2


def from_of(me, r, n):
    pairs = n // 2
    return ((me // 2 + pairs - r // 2) % pairs) * 2 + (me % 2 + r % 2) % 2


def after(value, *earlier):
    if isinstance(value, list):
        return [after(value[0], *earlier), *value[1:]]
    return lax.optimization_barrier((value, *earlier))[0] if earlier else value


class Flow:
    def __init__(self, depth, lag):
        self.depth, self.lag = depth, lag
        self.landed = {"px": [], "py": []}
        self.latest = []
        self.due = []

    def back(self, axis):
        landed, depth = self.landed[axis], self.depth[axis]
        return landed[max(0, len(landed) - 2 * depth + 1) : max(0, len(landed) - depth + 1)]

    def owe(self, kind, array):
        self.due.append((len(self.landed["px"]) + self.lag[kind], array))

    def work(self, function, s, value, *rest, back=True):
        out = function(s, after(value, *self.latest, *(self.back("px") if back else [])), *rest)
        self.latest = [jax.tree.leaves(out)[0]]
        if back:
            self.owe("work", self.latest[0])
        return out

    def settle(self, depth):
        self.due = [(0, array) for _, array in self.due] + [(0, array) for array in self.latest]
        self.depth["px"] = depth

    def permute(self, axis, block, pairs):
        count = len(self.landed["px"])
        if axis == "px":
            pins = self.back("px") + [array for when, array in self.due if when <= count]
            self.due = [(when, array) for when, array in self.due if when > count]
        else:
            pins = self.back("py") + self.back("px")[-1:]
        got = lax.ppermute(after(block, *pins), axis, pairs)
        self.landed[axis].append(got)
        if axis == "py":
            self.owe("py", got)
        return got


class Exchange:
    def __init__(self, flow, axis, blocks):
        self.flow, self.axis, self.blocks, self.n = flow, axis, blocks, len(blocks)
        self.got = [blocks[0]] + [None] * (self.n - 1)
        self.order = sorted(range(1, self.n), key=lambda r: (r % 2, abs(2 * (r // 2) - self.n // 2), r))
        self.left = list(self.order)

    def send(self, count):
        for r in self.left[:count]:
            pairs = [(device, to_of(device, r, self.n)) for device in range(self.n)]
            self.got[r] = self.flow.permute(self.axis, self.blocks[r], pairs)
        self.left = self.left[count:]
        return self

    def rest(self):
        return self.send(self.n).got


class Sizes:
    def __init__(self, field_shape, count_px, count_py):
        self.nx, self.ny = count_px, count_py
        self.a, self.b, self.c = field_shape
        self.full = self.a * count_px
        self.by = self.b // count_px
        self.ax = self.a // count_py
        self.yc = ROWS
        self.chunks = self.by // ROWS
        self.parts = [(k, slice(k * LANES, (k + 1) * LANES)) for k in range(self.c // LANES)]
        self.field_bytes = 4 * self.a * self.b * self.c


def turn_spec(s, part):
    return pl.BlockSpec((s.a, s.yc, LANES), lambda i: (0, 0, part))


def first_in(s, field, chunk, potential, z_turned, to_px):
    def kernel(to_ref, f_ref, w_ref, high_ref, low_ref, *rest):
        outs, held = rest[:-1], rest[-1]
        moved = half_of(w_ref[...]) * f_ref[...]
        moved = lines_times(moved.reshape(2 * ROWS * s.nx * s.yc, s.c), (high_ref, low_ref))
        held[...] = moved.reshape(2 * ROWS, s.nx, s.yc, s.c)
        for r, out in enumerate(outs):
            out[...] = held[:, to_ref[r]]

    block = pl.BlockSpec((2 * ROWS, s.nx, s.yc, s.c), lambda i: (i, 0, chunk, 0))
    out = pl.BlockSpec((2 * ROWS, s.yc, s.c), lambda i: (i, 0, 0))
    view = (s.a, s.nx, s.by, s.c)
    return call(
        kernel,
        "z_lines_by_px",
        (s.a // (2 * ROWS),),
        [table_spec(), block, block] + [whole_spec((s.c, s.c))] * 2,
        [out] * s.nx,
        [jax.ShapeDtypeStruct((s.a, s.yc, s.c), F32)] * s.nx,
        [pltpu.VMEM((2 * ROWS, s.nx, s.yc, s.c), F32)],
        6 * s.a * s.b * s.c * s.c // s.chunks,
        3 * s.field_bytes // s.chunks,
    )(to_px, field.reshape(view), potential.reshape(view), *z_turned)


def first_by_py(s, field, potential, z_turned, to_py):
    step = ROWS // 2

    def kernel(to_ref, f_ref, w_ref, high_ref, low_ref, *outs):
        for r in range(s.ny):
            q = to_ref[r]
            moved = half_of(w_ref[q]) * f_ref[q]
            moved = lines_times(moved.reshape(step * s.b, s.c), (high_ref, low_ref))
            outs[r][...] = moved.reshape(step, s.b, s.c)

    block = pl.BlockSpec((s.ny, step, s.b, s.c), lambda i: (0, i, 0, 0))
    out = pl.BlockSpec((step, s.b, s.c), lambda i: (i, 0, 0))
    view = (s.ny, s.ax, s.b, s.c)
    return call(
        kernel,
        "z_lines_by_py",
        (s.ax // step,),
        [table_spec(), block, block] + [whole_spec((s.c, s.c))] * 2,
        [out] * s.ny,
        [jax.ShapeDtypeStruct((s.ax, s.b, s.c), F32)] * s.ny,
        [],
        6 * s.a * s.b * s.c * s.c,
        3 * s.field_bytes,
    )(to_py, field.reshape(view), potential.reshape(view), *z_turned)


def x_lines_forward(s, got, matrix, from_px, to_px, to_py):
    def kernel(from_ref, to_ref, part_ref, high_ref, low_ref, *rest):
        count = len(s.parts) * s.nx
        ins, outs = rest[:count], rest[count:-2]
        lines, moved = rest[-2:]
        y = pl.program_id(0)
        for place in range(count):
            r, (_, lanes) = place // len(s.parts), s.parts[place % len(s.parts)]
            rows = ins[place].reshape(s.a * s.yc, LANES)
            lines[pl.ds(pl.multiple_of(from_ref[r] * s.a, s.a), s.a), lanes] = rows[pl.ds(y, s.a, stride=s.yc), :]
        moved[...] = times_lines((high_ref, low_ref), lines[...])
        for r in range(s.nx):
            for k in range(s.ny):
                at = pl.multiple_of(to_ref[r] * s.a + part_ref[k] * s.ax, s.ax)
                outs[r][k, 0] = moved[pl.ds(at, s.ax), :]

    parted = pl.BlockSpec((s.ny, 1, s.ax, s.c), lambda i: (0, i, 0, 0))
    return call(
        kernel,
        "x_lines_forward",
        (s.yc,),
        [table_spec()] * 3
        + [whole_spec((s.full, s.full))] * 2
        + [turn_spec(s, part) for _ in range(s.nx) for part, _ in s.parts],
        [parted] * s.nx,
        [jax.ShapeDtypeStruct((s.ny, s.yc, s.ax, s.c), F32)] * s.nx,
        [pltpu.VMEM((s.full, s.c), F32), pltpu.VMEM((s.full, s.c), F32)],
        6 * s.a * s.b * s.c * s.full // s.chunks,
        2 * s.field_bytes // s.chunks,
    )(from_px, to_px, to_py, *matrix, *[block for block in got for _ in s.parts])


def x_lines_adjoint(s, got, matrix, from_px, to_px, from_py):
    def kernel(from_ref, to_ref, part_ref, high_ref, low_ref, *rest):
        ins, outs = rest[: s.nx], rest[s.nx : -3]
        lines, moved, held = rest[-3:]
        y = pl.program_id(0)
        for r in range(s.nx):
            for k in range(s.ny):
                at = pl.multiple_of(from_ref[r] * s.a + part_ref[k] * s.ax, s.ax)
                lines[pl.ds(at, s.ax), :] = ins[r][k, 0]
        moved[...] = times_lines((high_ref, low_ref), lines[...])
        for r in range(s.nx):
            for part, lanes in s.parts:
                taken = moved[pl.ds(pl.multiple_of(to_ref[r] * s.a, s.a), s.a), lanes]
                held[part, r, pl.ds(y, s.a, stride=s.yc), :] = taken

        @pl.when(y == s.yc - 1)
        def _():
            for r in range(s.nx):
                for part, lanes in s.parts:
                    outs[r][:, :, lanes] = held[part, r].reshape(s.a, s.yc, LANES)

    parted = pl.BlockSpec((s.ny, 1, s.ax, s.c), lambda i: (0, i, 0, 0))
    return call(
        kernel,
        "x_lines_adjoint",
        (s.yc,),
        [table_spec()] * 3 + [whole_spec((s.full, s.full))] * 2 + [parted] * s.nx,
        [whole_spec((s.a, s.yc, s.c))] * s.nx,
        [jax.ShapeDtypeStruct((s.a, s.yc, s.c), F32)] * s.nx,
        [
            pltpu.VMEM((s.full, s.c), F32),
            pltpu.VMEM((s.full, s.c), F32),
            pltpu.VMEM((len(s.parts), s.nx, s.a * s.yc, LANES), F32),
        ],
        6 * s.a * s.b * s.c * s.full // s.chunks,
        2 * s.field_bytes // s.chunks,
    )(from_px, to_px, from_py, *matrix, *got)


def y_lines_unturned(s, got, matrix, from_px, from_py, to_py):
    def kernel(px_ref, from_ref, to_ref, high_ref, low_ref, *rest):
        count = len(s.parts) * s.chunks * s.ny
        ins, outs = rest[:count], rest[count:-2]
        lines, moved = rest[-2:]

        @pl.loop(0, ROWS)
        def _(x):
            for place in range(count):
                part, lanes = s.parts[place % len(s.parts)]
                k, chunk = place // len(s.parts) % s.ny, place // len(s.parts) // s.ny
                rows = ins[place].reshape(s.nx * s.yc * ROWS, LANES)
                taken = rows[pl.ds(x, s.nx * s.yc, stride=ROWS), :]
                for r in range(s.nx):
                    at = from_ref[k] * s.b + px_ref[r] * s.by + chunk * s.yc
                    lines[pl.ds(pl.multiple_of(at, s.yc), s.yc), lanes] = taken[r * s.yc : (r + 1) * s.yc]
            moved[...] = times_lines((high_ref, low_ref), lines[...])
            for k in range(s.ny):
                outs[k][x] = moved[pl.ds(pl.multiple_of(to_ref[k] * s.b, s.b), s.b), :]

    turned = [
        pl.BlockSpec((s.nx, s.yc, ROWS, LANES), functools.partial(lambda part, i: (0, 0, i, part), part))
        for part, _ in s.parts
    ]
    plain = pl.BlockSpec((ROWS, s.b, s.c), lambda i: (i, 0, 0))
    return call(
        kernel,
        "y_lines_unturned",
        (s.ax // ROWS,),
        [table_spec()] * 3 + [whole_spec((s.full, s.full))] * 2 + turned * (s.chunks * s.ny),
        [plain] * s.ny,
        [jax.ShapeDtypeStruct((s.ax, s.b, s.c), F32)] * s.ny,
        [pltpu.VMEM((s.full, s.c), F32), pltpu.VMEM((s.full, s.c), F32)],
        6 * s.a * s.b * s.c * s.full,
        2 * s.field_bytes,
    )(from_px, from_py, to_py, *matrix, *[block for chunk in got for block in chunk for _ in s.parts])


def y_lines_turned(s, got, matrix, to_px, from_py, to_py):
    def kernel(px_ref, from_ref, to_ref, high_ref, low_ref, *rest):
        ins, outs = rest[: s.ny], rest[s.ny : -3]
        lines, moved, held = rest[-3:]

        @pl.loop(0, ROWS)
        def _(x):
            for k in range(s.ny):
                lines[pl.ds(pl.multiple_of(from_ref[k] * s.b, s.b), s.b), :] = ins[k][x]
            moved[...] = times_lines((high_ref, low_ref), lines[...])
            for chunk in range(s.chunks):
                for k in range(s.ny):
                    for r in range(s.nx):
                        at = to_ref[k] * s.b + px_ref[r] * s.by + chunk * s.yc
                        taken = moved[pl.ds(pl.multiple_of(at, s.yc), s.yc), :]
                        for part, lanes in s.parts:
                            place = pl.ds(x + r * s.yc * ROWS, s.yc, stride=ROWS)
                            held[part, chunk * s.ny + k, place, :] = taken[:, lanes]

        for place, out in enumerate(outs):
            for part, lanes in s.parts:
                out[:, :, :, lanes] = held[part, place].reshape(s.nx, s.yc, ROWS, LANES)

    turned = pl.BlockSpec((s.nx, s.yc, ROWS, s.c), lambda i: (0, 0, i, 0))
    plain = pl.BlockSpec((ROWS, s.b, s.c), lambda i: (i, 0, 0))
    outs = call(
        kernel,
        "y_lines_turned",
        (s.ax // ROWS,),
        [table_spec()] * 3 + [whole_spec((s.full, s.full))] * 2 + [plain] * s.ny,
        [turned] * (s.chunks * s.ny),
        [jax.ShapeDtypeStruct((s.nx, s.yc, s.ax, s.c), F32)] * (s.chunks * s.ny),
        [
            pltpu.VMEM((s.full, s.c), F32),
            pltpu.VMEM((s.full, s.c), F32),
            pltpu.VMEM((len(s.parts), s.chunks * s.ny, s.nx * s.yc * ROWS, LANES), F32),
        ],
        6 * s.a * s.b * s.c * s.full,
        2 * s.field_bytes,
    )(to_px, from_py, to_py, *matrix, *got)
    return [outs[chunk * s.ny : (chunk + 1) * s.ny] for chunk in range(s.chunks)]


def finish_forward(s, got, potential, end_adjoint, from_py):
    step = ROWS // 2

    def kernel(from_ref, w_ref, e_ref, *rest):
        ins, (final_ref, term_ref) = rest[: s.ny], rest[s.ny :]
        for k in range(s.ny):
            q = from_ref[k]
            final = half_of(w_ref[q]) * ins[k][...]
            final_ref[q] = final
            term_ref[q] = 0.05 * final * e_ref[q]

    block = pl.BlockSpec((s.ny, step, s.b, s.c), lambda i: (0, i, 0, 0))
    plain = pl.BlockSpec((step, s.b, s.c), lambda i: (i, 0, 0))
    view = (s.ny, s.ax, s.b, s.c)
    outs = call(
        kernel,
        "finish_forward",
        (s.ax // step,),
        [table_spec(), block, block] + [plain] * s.ny,
        [block, block],
        [jax.ShapeDtypeStruct(view, F32)] * 2,
        [],
        s.a * s.b * s.c * 4,
        5 * s.field_bytes,
    )(from_py, potential.reshape(view), end_adjoint.reshape(view), *got)
    return [out.reshape(s.a, s.b, s.c) for out in outs]


def finish_adjoint(s, got, chunk, potential, start_field, density, first, from_px):
    def kernel(from_ref, w_ref, f_ref, term_ref, *rest):
        ins, (first_ref, density_ref) = rest[: s.nx], rest[-2:]
        for r in range(s.nx):
            p = from_ref[r]
            value = half_of(w_ref[:, p]) * ins[r][...]
            first_ref[:, p] = value
            density_ref[:, p] = term_ref[:, p] + 0.05 * f_ref[:, p] * value

    view = (s.a, s.nx, s.by, s.c)
    block = pl.BlockSpec((2 * ROWS, s.nx, s.yc, s.c), lambda i: (i, 0, chunk, 0))
    plain = pl.BlockSpec((2 * ROWS, s.yc, s.c), lambda i: (i, 0, 0))
    outs = call(
        kernel,
        "finish_adjoint",
        (s.a // (2 * ROWS),),
        [table_spec(), block, block, block] + [plain] * s.nx,
        [block, block],
        [jax.ShapeDtypeStruct(view, F32)] * 2,
        [],
        s.a * s.b * s.c * 4 // s.chunks,
        6 * s.field_bytes // s.chunks,
        {3: 1},
    )(from_px, potential.reshape(view), start_field.reshape(view), density.reshape(view), *got)
    return [out.reshape(s.a, s.b, s.c) for out in outs]


def finish_block(s, got, chunk, potential, start_field, density, first, source):
    def kernel(source_ref, got_ref, w_ref, f_ref, term_ref, whole_ref, first_ref, density_ref):
        value = half_of(w_ref[...]) * got_ref[...].reshape(w_ref.shape)
        first_ref[...] = value
        density_ref[...] = term_ref[...] + 0.05 * f_ref[...] * value

    step = s.a // 2
    view = (s.a, s.nx, s.by, s.c)
    block = pl.BlockSpec((step, 1, s.yc, s.c), lambda i, source_ref: (i, source_ref[0], chunk, 0))
    touched = 6 * s.field_bytes // s.chunks // s.nx
    outs = pl.pallas_call(
        kernel,
        name="finish_block",
        grid_spec=pltpu.PrefetchScalarGridSpec(
            num_scalar_prefetch=1,
            grid=(s.a // step,),
            in_specs=[pl.BlockSpec((step, s.yc, s.c), lambda i, source_ref: (i, 0, 0))]
            + [block] * 3
            + [pl.BlockSpec(memory_space=pl.ANY)],
            out_specs=[block, block],
        ),
        out_shape=[jax.ShapeDtypeStruct(view, F32)] * 2,
        input_output_aliases={4: 1, 5: 0},
        cost_estimate=pl.CostEstimate(flops=0, bytes_accessed=touched, transcendentals=0),
        compiler_params=pltpu.CompilerParams(vmem_limit_bytes=VMEM_LIMIT),
    )(source, got, *(array.reshape(view) for array in (potential, start_field, density, first)))
    return [out.reshape(s.a, s.b, s.c) for out in outs]


def gather(s, blocks, count):
    return [jnp.stack([block[r] for block in blocks]) for r in range(count)]


def tiled_body(s, start_field, end_adjoint, potential, line_xy, line_z):
    me_px, me_py = lax.axis_index("px"), lax.axis_index("py")
    to_px, from_px = (f(me_px, jnp.arange(s.nx, dtype=jnp.int32), s.nx) for f in (to_of, from_of))
    to_py, from_py = (f(me_py, jnp.arange(s.ny, dtype=jnp.int32), s.ny) for f in (to_of, from_of))
    xy, xy_turned, z, z_turned = (two_parts(m) for m in (line_xy, line_xy.T, line_z, line_z.T))

    flow = Flow({"px": 4, "py": 3}, {"work": 4, "py": 12})
    px, py = functools.partial(Exchange, flow, "px"), functools.partial(Exchange, flow, "py")
    last = s.chunks - 1

    f_in = [px(flow.work(first_in, s, start_field, 0, potential, z_turned, to_px)).send(2)]
    for chunk in range(1, s.chunks):
        f_in.append(px(flow.work(first_in, s, start_field, chunk, potential, z_turned, to_px)))
    f_in[0].send(3)
    a_in = py(flow.work(first_by_py, s, end_adjoint, potential, z, to_py))
    a_in.send(1)
    f_in[0].rest()
    for chunk in range(1, s.chunks):
        f_in[chunk].send(1)
        a_in.send(1)
        f_in[chunk].send(1)
    f_out = [px(flow.work(x_lines_forward, s, f_in[0].rest(), xy, from_px, to_px, to_py))]
    f_in[last].send(2)
    adjoint = a_in.rest()
    for stage in f_in:
        stage.rest()
    f_out[0].send(4)
    for chunk in range(1, s.chunks):
        f_out.append(px(flow.work(x_lines_forward, s, f_in[chunk].rest(), xy, from_px, to_px, to_py)))
    adjoint = flow.work(y_lines_turned, s, adjoint, xy_turned, to_px, from_py, to_py)
    a_back = [py(blocks) for blocks in adjoint]

    for chunk in range(s.chunks):
        a_back[chunk].send(1)
        f_out[chunk].send(1)
        a_back[chunk].send(1)
        f_out[chunk].send(2)
        a_back[chunk].send(1)
        if chunk < last:
            f_out[chunk].rest()
    f_out[last].send(1)
    a_in = [px(flow.work(gather, s, a_back[0].rest(), s.nx))]
    f_in = [py(flow.work(gather, s, f_out[0].got, s.ny))]
    f_in[0].send(1)
    f_out[last].send(2)
    f_in[0].send(1)
    for chunk in range(1, s.chunks):
        a_in.append(px(flow.work(gather, s, a_back[chunk].rest(), s.nx)))
    f_out[last].rest()
    f_in[0].send(1)
    a_in[0].send(3)

    for chunk in range(1, s.chunks):
        f_in.append(py(flow.work(gather, s, f_out[chunk].got, s.ny)))
    f_in[last].send(1)
    a_in[0].send(2)
    f_in[last].send(1)
    a_in[0].rest()
    f_in[last].rest()
    a_in[last].send(3)
    forward = [stage.rest() for stage in f_in]
    f_back = py(flow.work(y_lines_unturned, s, forward, xy, from_px, from_py, to_py))
    a_out = [px(flow.work(x_lines_adjoint, s, a_in[0].rest(), xy_turned, from_px, to_px, from_py))]
    a_in[last].send(2)
    f_back.send(1)
    for stage in a_in:
        stage.rest()
    a_out[0].send(2)
    f_back.send(1)
    a_out[0].send(2)
    f_back.rest()
    for chunk in range(1, s.chunks):
        a_out.append(px(flow.work(x_lines_adjoint, s, a_in[chunk].rest(), xy_turned, from_px, to_px, from_py)))
    a_out[0].send(3)
    final, density = flow.work(finish_forward, s, f_back.rest(), potential, end_adjoint, from_py, back=False)
    a_out[0].rest()
    a_out[last].send(3)
    args = (0, potential, start_field, density, None, from_px)
    first, density = flow.work(finish_adjoint, s, a_out[0].rest(), *args, back=False)
    for chunk in range(1, s.chunks):
        a_out[chunk].send(len(a_out[chunk].left) - 3)
        flow.settle(4)
        a_out[chunk].rest()
        for r in [0, *a_out[chunk].order]:
            args = (chunk, potential, start_field, density, first, from_px[r : r + 1])
            first, density = finish_block(s, a_out[chunk].got[r], *args)
    return final, first, density


def plain_body(s, start_field, end_adjoint, potential, line_xy, line_z):
    half = half_of(potential)

    def step(field, matrix_xy, matrix_z):
        lines = product(half * field, matrix_z.T)
        lines = lax.all_to_all(lines, "px", 1, 0, tiled=True)
        lines = product(matrix_xy, lines.reshape(s.full, -1)).reshape(lines.shape)
        lines = lax.all_to_all(lines, "px", 0, 1, tiled=True)
        lines = lax.all_to_all(lines, "py", 0, 1, tiled=True)
        lines = jnp.einsum("ij,ajc->aic", matrix_xy, lines, precision=lax.Precision.HIGHEST)
        return half * lax.all_to_all(lines, "py", 1, 0, tiled=True)

    final = step(start_field, line_xy, line_z)
    first = step(end_adjoint, line_xy.T, line_z.T)
    return final, first, 0.05 * start_field * first + 0.05 * final * end_adjoint


def body(start_field, end_adjoint, potential, line_xy, line_z):
    s = Sizes(start_field.shape, lax.axis_size("px"), lax.axis_size("py"))
    even = s.nx % 2 == 0 and s.ny % 2 == 0
    whole_tiles = s.by % ROWS == 0 and s.ax % ROWS == 0 and s.c % 128 == 0
    run = tiled_body if even and whole_tiles and s.by and s.ax else plain_body
    return run(s, start_field, end_adjoint, potential, line_xy, line_z)


def solution(mesh):
    placed = (P("px", "py", None), P("px", "py", None), P("px", "py", None), P(), P())
    return jax.shard_map(
        body,
        mesh=mesh,
        in_specs=placed,
        out_specs=(P("px", "py", None), P("px", "py", None), P("px", "py", None)),
        check_vma=False,
    )
```

time: 1690 us -> 788 us (0.47)
  other arithmetic: 714 us -> 8.33 us
  local copies, waits for them, and re-layouts: 572 us -> 6.34 us
  waiting for transfers between devices: 219 us -> 490 us
  Pallas kernels: 0 us -> 149 us
  matrix products: 120 us -> 0 us
  starting transfers between devices: 50.7 us -> 131 us
    unnamed x4 -> x0, other arithmetic: 586 us -> none
    ppermute x0 -> x74, waiting for transfers between devices: none -> 490 us  [permute(): got = lax.ppermute(after(block, *pins), axis, pairs)]
    unnamed x22 -> x114, local copies, waits for them, and re-layouts: 282 us -> 3.72 us
    all_to_all x8 -> x0, waiting for transfers between devices: 219 us -> none  [the longest x2 83.3 us: y_to_z(): got = lax.all_to_all(send, 'py', split_axis=1, concat_axis=4, tiled=True)]
    pallas_call x0 -> x19, Pallas kernels: none -> 149 us  [the longest x8 24.4 us: finish_block(): pl.pallas_call(kernel, name='finish_block', grid_spec=pltpu.PrefetchScala...]
    ppermute x0 -> x74, starting transfers between devices: none -> 131 us  [permute(): got = lax.ppermute(after(block, *pins), axis, pairs)]
    reshape x8 -> x0, local copies, waits for them, and re-layouts: 130 us -> none  [the longest x4 57.4 us: y_to_z(): send = stacked.reshape(fields, count_py, cells_y, cells_x, block_z)]
    dot_general x6 -> x0, matrix products: 120 us -> none  [product(): jnp.dot(left, right, precision=lax.Precision.HIGHEST, preferred_element_t...]
  transfers between devices with their start and end apart: 8 -> 74, of which waited for: 3 -> 44; matrix products, arithmetic and copies ran while one was open for 78% -> 1% of each run, Pallas kernels for 0% -> 18%
where the time goes in v1:
time: 788 us; the launch traced here: 787 us
  waiting for transfers between devices  490 us (62%)
  Pallas kernels  149 us (19%)
  starting transfers between devices  131 us (17%)
  other arithmetic  8.33 us (1%)
    ppermute x74, waiting for transfers between devices, permute(): got = lax.ppermute(after(block, *pins), axis, pairs)  490 us
    ppermute x74, starting transfers between devices, permute(): got = lax.ppermute(after(block, *pins), axis, pairs)  131 us
    pallas_call x8, Pallas kernels, finish_block(): pl.pallas_call(kernel, name='finish_block', grid_spec=pltpu.PrefetchScala...  24.4 us
    pallas_call x2, Pallas kernels, x_lines_adjoint(): call(kernel, 'x_lines_adjoint', (s.yc,), [table_spec()] * 3 + [whole_spec...  22.4 us
    pallas_call x2, Pallas kernels, x_lines_forward(): call(kernel, 'x_lines_forward', (s.yc,), [table_spec()] * 3 + [whole_spec...  20.6 us
    pallas_call x1, Pallas kernels, y_lines_turned(): call(kernel, 'y_lines_turned', (s.ax // ROWS,), [table_spec()] * 3 + [who...  17.8 us
    pallas_call x1, Pallas kernels, y_lines_unturned(): call(kernel, 'y_lines_unturned', (s.ax // ROWS,), [table_spec()] * 3 + [w...  16.8 us
  transfers between devices with their start and end apart: 74, of which 44 were waited for; matrix products, arithmetic and copies ran while one was open for 1% of the time, Pallas kernels for 18%

profile of v1, /device:TPU:12, one launch (start us, length us, event | category | flops | bytes accessed | tf_op | source)
XLA Modules:
  0.0 786.8 jit_solution(15416106745224003873)
XLA Ops:
  23.1 13.0 %collective-permute-done.rest_8_.rest_9_ = f32[64,8,256]{2,1,0:T(8,128)S(1)} collective-permute-done((f32[64,8,256]{2,1,0:T(8,128)}, f32[64,8,256]{2,1,0:T(8,128)S(1)}, u32[]{:S(2)}, u32[]{:S(2)}) %collective-permute-start) | collective-permute-done | bytes 524320 | tf_op jit(solution)/shard_map/ppermute | solution.py:121
  36.1 12.5 %collective-permute-start.4 = (f32[64,8,256]{2,1,0:T(8,128)}, f32[64,8,256]{2,1,0:T(8,128)}, u32[]{:S(2)}, u32[]{:S(2)}) collective-permute-start(f32[64,8,256]{2,1,0:T(8,128)} %get-tuple-element.181), channel_id=1, source_target_pairs={{0,12},{4,8},{8,20},{12,16},{16,28},{20,24},{24,4},{28,0},{1,13},{... | collective-permute-start | bytes 1572872 | tf_op jit(solution)/shard_map/ppermute | solution.py:121
  48.6 21.2 %collective-permute-done.1.rest_4_.rest_5_ = f32[64,8,256]{2,1,0:T(8,128)S(1)} collective-permute-done((f32[64,8,256]{2,1,0:T(8,128)}, f32[64,8,256]{2,1,0:T(8,128)S(1)}, u32[]{:S(2)}, u32[]{:S(2)}) %collective-permute-start.1) | collective-permute-done | bytes 524320 | tf_op jit(solution)/shard_map/ppermute | solution.py:121
  69.8 11.4 %collective-permute-done.2.rest_12_.rest_13_ = f32[64,8,256]{2,1,0:T(8,128)} collective-permute-done((f32[64,8,256]{2,1,0:T(8,128)}, f32[64,8,256]{2,1,0:T(8,128)}, u32[]{:S(2)}, u32[]{:S(2)}) %collective-permute-start.2) | collective-permute-done | bytes 524320 | tf_op jit(solution)/shard_map/ppermute | solution.py:121
  95.7 18.2 %collective-permute-done.4.rest_6_.rest_7_ = f32[64,8,256]{2,1,0:T(8,128)} collective-permute-done((f32[64,8,256]{2,1,0:T(8,128)}, f32[64,8,256]{2,1,0:T(8,128)}, u32[]{:S(2)}, u32[]{:S(2)}) %collective-permute-start.4) | collective-permute-done | bytes 524320 | tf_op jit(solution)/shard_map/ppermute | solution.py:121
  118.8 17.4 %collective-permute-done.7.rest_8_.rest_9_ = f32[64,8,256]{2,1,0:T(8,128)S(1)} collective-permute-done((f32[64,8,256]{2,1,0:T(8,128)S(1)}, f32[64,8,256]{2,1,0:T(8,128)S(1)}, u32[]{:S(2)}, u32[]{:S(2)}) %collective-permute-start.7) | collective-permute-done | bytes 524320 | tf_op jit(solution)/shard_map/ppermute | solution.py:121
  136.3 22.4 %collective-permute-done.13.rest_10_.rest_11_ = f32[64,8,256]{2,1,0:T(8,128)S(1)} collective-permute-done((f32[64,8,256]{2,1,0:T(8,128)S(1)}, f32[64,8,256]{2,1,0:T(8,128)S(1)}, u32[]{:S(2)}, u32[]{:S(2)}) %collective-permute-start.13) | collective-permute-done | bytes 524320 | tf_op jit(solution)/shard_map/ppermute | solution.py:121
  223.1 15.1 %collective-permute-start.23 = (f32[4,8,16,256]{3,2,1,0:T(8,128)}, f32[4,8,16,256]{3,2,1,0:T(8,128)S(1)}, u32[]{:S(2)}, u32[]{:S(2)}) collective-permute-start(f32[4,8,16,256]{3,2,1,0:T(8,128)} %get-tuple-element.226), channel_id=1, source_target_pairs={{0,20},{4,16},{8,28},{12,24},{16,4},{20,0},{24,12},{28,8},{1,21},{... | collective-permute-start | bytes 1572872 | tf_op jit(solution)/shard_map/ppermute | solution.py:121
  239.3 17.1 %collective-permute-done.19 = f32[4,8,16,256]{3,2,1,0:T(8,128)S(1)} collective-permute-done((f32[4,8,16,256]{3,2,1,0:T(8,128)}, f32[4,8,16,256]{3,2,1,0:T(8,128)S(1)}, u32[]{:S(2)}, u32[]{:S(2)}) %collective-permute-start.19) | collective-permute-done | bytes 524320 | tf_op jit(solution)/shard_map/ppermute | solution.py:121
  283.2 17.8 %y_lines_turned.1 = (f32[8,8,16,256]{3,2,1,0:T(8,128)}, f32[8,8,16,256]{3,2,1,0:T(8,128)}, f32[8,8,16,256]{3,2,1,0:T(8,128)}, f32[8,8,16,256]{3,2,1,0:T(8,128)},...) custom-call(s32[8]{0:T(128)} %fusion.13.to_ref.px_ref, ...), custom_call_target="tpu_custom_call" | custom-call | flops 6442450944 | bytes 16777216 | tf_op jit(solution)/shard_map/y_lines_turned/pallas_call | solution.py:348
  305.9 18.9 %collective-permute-done.24 = f32[4,8,16,256]{3,2,1,0:T(8,128)S(1)} collective-permute-done((f32[4,8,16,256]{3,2,1,0:T(8,128)}, f32[4,8,16,256]{3,2,1,0:T(8,128)S(1)}, u32[]{:S(2)}, u32[]{:S(2)}) %collective-permute-start.24) | collective-permute-done | bytes 524320 | tf_op jit(solution)/shard_map/ppermute | solution.py:121
  359.0 21.7 %collective-permute-done.34 = f32[4,8,16,256]{3,2,1,0:T(8,128)S(1)} collective-permute-done((f32[4,8,16,256]{3,2,1,0:T(8,128)}, f32[4,8,16,256]{3,2,1,0:T(8,128)S(1)}, u32[]{:S(2)}, u32[]{:S(2)}) %collective-permute-start.34) | collective-permute-done | bytes 524320 | tf_op jit(solution)/shard_map/ppermute | solution.py:121
  395.8 22.9 %collective-permute-done.38.rest_4_ = f32[4,8,16,256]{3,2,1,0:T(8,128)S(1)} collective-permute-done((f32[4,8,16,256]{3,2,1,0:T(8,128)S(1)}, f32[4,8,16,256]{3,2,1,0:T(8,128)S(1)}, u32[]{:S(2)}, u32[]{:S(2)}) %collective-permute-start.38) | collective-permute-done | bytes 524320 | tf_op jit(solution)/shard_map/ppermute | solution.py:121
  448.1 19.4 %collective-permute-done.46.rest_6_.rest_7_ = f32[8,8,16,256]{3,2,1,0:T(8,128)S(1)} collective-permute-done((f32[8,8,16,256]{3,2,1,0:T(8,128)S(1)}, f32[8,8,16,256]{3,2,1,0:T(8,128)S(1)}, u32[]{:S(2)}, u32[]{:S(2)}) %collective-permute-start.46) | collective-permute-done | bytes 1048608 | tf_op jit(solution)/shard_map/ppermute | solution.py:121
  497.0 28.2 %collective-permute-done.50.rest_4_ = f32[4,8,16,256]{3,2,1,0:T(8,128)S(1)} collective-permute-done((f32[4,8,16,256]{3,2,1,0:T(8,128)S(1)}, f32[4,8,16,256]{3,2,1,0:T(8,128)S(1)}, u32[]{:S(2)}, u32[]{:S(2)}) %collective-permute-start.50) | collective-permute-done | bytes 524320 | tf_op jit(solution)/shard_map/ppermute | solution.py:121
  532.0 16.8 %y_lines_unturned.1 = (f32[16,128,256]{2,1,0:T(8,128)}, f32[16,128,256]{2,1,0:T(8,128)}, f32[16,128,256]{2,1,0:T(8,128)}, f32[16,128,256]{2,1,0:T(8,128)}) custom-call(s32[8]{0:T(128)} %fusion.9.from_ref.px_ref, s32[4]{0:T(128)} %fusion.7.from_ref.part_ref, s32[4]{0:T(128)} %fusion.11.to_ref.part_ref, bf16[512,512]{1,0:T(8,128)(2,1)} %get-tuple-element.406.high_ref, ...), custom_call_target="tpu_custom_call" | custom-call | flops 6442450944 | bytes 16777216 | tf_op jit(solution)/shard_map/y_lines_unturned/pallas_call | solution.py:310
  563.5 20.9 %collective-permute-done.53.rest_7_ = f32[4,8,16,256]{3,2,1,0:T(8,128)} collective-permute-done((f32[4,8,16,256]{3,2,1,0:T(8,128)S(1)}, f32[4,8,16,256]{3,2,1,0:T(8,128)}, u32[]{:S(2)}, u32[]{:S(2)}) %collective-permute-start.53) | collective-permute-done | bytes 524320 | tf_op jit(solution)/shard_map/ppermute | solution.py:121
  611.3 15.5 %collective-permute-done.61.rest_2_ = f32[64,8,256]{2,1,0:T(8,128)S(1)} collective-permute-done((f32[64,8,256]{2,1,0:T(8,128)}, f32[64,8,256]{2,1,0:T(8,128)S(1)}, u32[]{:S(2)}, u32[]{:S(2)}) %collective-permute-start.61) | collective-permute-done | bytes 524320 | tf_op jit(solution)/shard_map/ppermute | solution.py:121
  660.4 12.0 %collective-permute-done.68.rest_7_ = f32[64,8,256]{2,1,0:T(8,128)} collective-permute-done((f32[64,8,256]{2,1,0:T(8,128)}, f32[64,8,256]{2,1,0:T(8,128)}, u32[]{:S(2)}, u32[]{:S(2)}) %collective-permute-start.68) | collective-permute-done | bytes 524320 | tf_op jit(solution)/shard_map/ppermute | solution.py:121
  674.4 16.2 %collective-permute-done.65.got_ref = f32[64,8,256]{2,1,0:T(8,128)S(1)} collective-permute-done((f32[64,8,256]{2,1,0:T(8,128)}, f32[64,8,256]{2,1,0:T(8,128)S(1)}, u32[]{:S(2)}, u32[]{:S(2)}) %collective-permute-start.65) | collective-permute-done | bytes 524320 | tf_op jit(solution)/shard_map/ppermute | solution.py:121
  694.8 14.9 %collective-permute-start.72 = (f32[64,8,256]{2,1,0:T(8,128)}, f32[64,8,256]{2,1,0:T(8,128)}, u32[]{:S(2)}, u32[]{:S(2)}) collective-permute-start(f32[64,8,256]{2,1,0:T(8,128)} %get-tuple-element.316), channel_id=1, source_target_pairs={{0,12},{4,8},{8,20},{12,16},{16,28},{20,24},{24,4},{28,0},{1,13},{... | collective-permute-start | bytes 1572872 | tf_op jit(solution)/shard_map/ppermute | solution.py:121
  709.7 13.3 %collective-permute-done.67.got_ref = f32[64,8,256]{2,1,0:T(8,128)} collective-permute-done((f32[64,8,256]{2,1,0:T(8,128)}, f32[64,8,256]{2,1,0:T(8,128)}, u32[]{:S(2)}, u32[]{:S(2)}) %collective-permute-start.67) | collective-permute-done | bytes 524320 | tf_op jit(solution)/shard_map/ppermute | solution.py:121
  722.9 14.8 %collective-permute-done.69.got_ref = f32[64,8,256]{2,1,0:T(8,128)} collective-permute-done((f32[64,8,256]{2,1,0:T(8,128)}, f32[64,8,256]{2,1,0:T(8,128)}, u32[]{:S(2)}, u32[]{:S(2)}) %collective-permute-start.69) | collective-permute-done | bytes 524320 | tf_op jit(solution)/shard_map/ppermute | solution.py:121
  739.2 14.0 %finish_forward.1 = (f32[4,16,128,256]{3,2,1,0:T(8,128)}, f32[4,16,128,256]{3,2,1,0:T(8,128)}) custom-call(s32[4]{0:T(128)} %fusion.7.from_ref.part_ref, f32[4,16,128,256]{3,2,1,0:T(8,128)} %bitcast.19, f32[4,16,128,256]{3,2,1,0:T(8,128)} %bitcast.44, f32[16,128,256]{2,1,0:T(8,128)} %get-tuple-element.285.rest_0_, f32[16,128,256]{2,1,0:T(8,128)} %copy-done.3, ...), custom_call_target="tpu_custom_call" | custom-call | flops 8388608 | bytes 41943040 | tf_op jit(solution)/shard_map/finish_forward/pallas_call | solution.py:380
  (292 shorter events, 369.7 us)
Async XLA Ops:
  12.5 57.2 %collective-permute-start.1 = (f32[64,8,256]{2,1,0:T(8,128)}, f32[64,8,256]{2,1,0:T(8,128)S(1)}, u32[]{:S(2)}, u32[]{:S(2)}) collective-permute-start(f32[64,8,256]{2,1,0:T(8,128)} %get-tuple-element.175), channel_id=1, source_target_pairs={{0,8},{4,12},{8,16},{12,20},{16,24},{20,28},{24,0},{28,4},{1,9},{5... | collective-permute-start | bytes 1572872 | tf_op jit(solution)/shard_map/ppermute | solution.py:121
  12.5 68.6 %collective-permute-start.2 = (f32[64,8,256]{2,1,0:T(8,128)}, f32[64,8,256]{2,1,0:T(8,128)}, u32[]{:S(2)}, u32[]{:S(2)}) collective-permute-start(f32[64,8,256]{2,1,0:T(8,128)} %get-tuple-element.178), channel_id=1, source_target_pairs={{0,24},{4,28},{8,0},{12,4},{16,8},{20,12},{24,16},{28,20},{1,25},{... | collective-permute-start | bytes 1572872 | tf_op jit(solution)/shard_map/ppermute | solution.py:121
  14.5 80.4 %collective-permute-start.3 = (f32[64,8,256]{2,1,0:T(8,128)}, f32[64,8,256]{2,1,0:T(8,128)}, u32[]{:S(2)}, u32[]{:S(2)}) collective-permute-start(f32[64,8,256]{2,1,0:T(8,128)} %get-tuple-element.179), channel_id=1, source_target_pairs={{0,20},{4,16},{8,28},{12,24},{16,4},{20,0},{24,12},{28,8},{1,21},{... | collective-permute-start | bytes 1572872 | tf_op jit(solution)/shard_map/ppermute | solution.py:121
  36.1 77.8 %collective-permute-start.4 = (f32[64,8,256]{2,1,0:T(8,128)}, f32[64,8,256]{2,1,0:T(8,128)}, u32[]{:S(2)}, u32[]{:S(2)}) collective-permute-start(f32[64,8,256]{2,1,0:T(8,128)} %get-tuple-element.181), channel_id=1, source_target_pairs={{0,12},{4,8},{8,20},{12,16},{16,28},{20,24},{24,4},{28,0},{1,13},{... | collective-permute-start | bytes 1572872 | tf_op jit(solution)/shard_map/ppermute | solution.py:121
  94.3 119.7 %collective-permute-start.16 = (f32[16,128,256]{2,1,0:T(8,128)}, f32[16,128,256]{2,1,0:T(8,128)}, u32[]{:S(2)}, u32[]{:S(2)}) collective-permute-start(f32[16,128,256]{2,1,0:T(8,128)} %get-tuple-element.210), channel_id=1, source_target_pairs={{0,2},{1,3},{2,0},{3,1},{4,6},{5,7},{6,4},{7,5},{8,10},{9,11},{10,... | collective-permute-start | bytes 6291464 | tf_op jit(solution)/shard_map/ppermute | solution.py:121
  117.4 63.8 %collective-permute-start.11 = (f32[64,8,256]{2,1,0:T(8,128)}, f32[64,8,256]{2,1,0:T(8,128)}, u32[]{:S(2)}, u32[]{:S(2)}) collective-permute-start(f32[64,8,256]{2,1,0:T(8,128)} %get-tuple-element.198), channel_id=1, source_target_pairs={{0,24},{4,28},{8,0},{12,4},{16,8},{20,12},{24,16},{28,20},{1,25},{... | collective-permute-start | bytes 1572872 | tf_op jit(solution)/shard_map/ppermute | solution.py:121
  136.3 133.8 %collective-permute-start.17 = (f32[16,128,256]{2,1,0:T(8,128)}, f32[16,128,256]{2,1,0:T(8,128)}, u32[]{:S(2)}, u32[]{:S(2)}) collective-permute-start(f32[16,128,256]{2,1,0:T(8,128)} %get-tuple-element.212), channel_id=1, source_target_pairs={{0,3},{1,2},{2,1},{3,0},{4,7},{5,6},{6,5},{7,4},{8,11},{9,10},{10,... | collective-permute-start | bytes 6291464 | tf_op jit(solution)/shard_map/ppermute | solution.py:121
  158.8 124.4 %collective-permute-start.15 = (f32[16,128,256]{2,1,0:T(8,128)}, f32[16,128,256]{2,1,0:T(8,128)}, u32[]{:S(2)}, u32[]{:S(2)}) collective-permute-start(f32[16,128,256]{2,1,0:T(8,128)} %get-tuple-element.208), channel_id=1, source_target_pairs={{0,1},{1,0},{2,3},{3,2},{4,5},{5,4},{6,7},{7,6},{8,9},{9,8},{10,11... | collective-permute-start | bytes 6291464 | tf_op jit(solution)/shard_map/ppermute | solution.py:121
  214.0 56.0 %collective-permute-start.21 = (f32[4,8,16,256]{3,2,1,0:T(8,128)}, f32[4,8,16,256]{3,2,1,0:T(8,128)S(1)}, u32[]{:S(2)}, u32[]{:S(2)}) collective-permute-start(f32[4,8,16,256]{3,2,1,0:T(8,128)} %get-tuple-element.222), channel_id=1, source_target_pairs={{0,24},{4,28},{8,0},{12,4},{16,8},{20,12},{24,16},{28,20},{1,25},{... | collective-permute-start | bytes 1572872 | tf_op jit(solution)/shard_map/ppermute | solution.py:121
  223.1 55.8 %collective-permute-start.23 = (f32[4,8,16,256]{3,2,1,0:T(8,128)}, f32[4,8,16,256]{3,2,1,0:T(8,128)S(1)}, u32[]{:S(2)}, u32[]{:S(2)}) collective-permute-start(f32[4,8,16,256]{3,2,1,0:T(8,128)} %get-tuple-element.226), channel_id=1, source_target_pairs={{0,20},{4,16},{8,28},{12,24},{16,4},{20,0},{24,12},{28,8},{1,21},{... | collective-permute-start | bytes 1572872 | tf_op jit(solution)/shard_map/ppermute | solution.py:121
  347.3 71.4 %collective-permute-start.31 = (f32[8,8,16,256]{3,2,1,0:T(8,128)}, f32[8,8,16,256]{3,2,1,0:T(8,128)S(1)}, u32[]{:S(2)}, u32[]{:S(2)}) collective-permute-start(f32[8,8,16,256]{3,2,1,0:T(8,128)} %get-tuple-element.245), channel_id=1, source_target_pairs={{0,2},{1,3},{2,0},{3,1},{4,6},{5,7},{6,4},{7,5},{8,10},{9,11},{10,... | collective-permute-start | bytes 3145736 | tf_op jit(solution)/shard_map/ppermute | solution.py:121
  349.9 68.9 %collective-permute-start.32 = (f32[8,8,16,256]{3,2,1,0:T(8,128)}, f32[8,8,16,256]{3,2,1,0:T(8,128)S(1)}, u32[]{:S(2)}, u32[]{:S(2)}) collective-permute-start(f32[8,8,16,256]{3,2,1,0:T(8,128)} %get-tuple-element.247), channel_id=1, source_target_pairs={{0,3},{1,2},{2,1},{3,0},{4,7},{5,6},{6,5},{7,4},{8,11},{9,10},{10,... | collective-permute-start | bytes 3145736 | tf_op jit(solution)/shard_map/ppermute | solution.py:121
  358.8 59.9 %collective-permute-start.30 = (f32[8,8,16,256]{3,2,1,0:T(8,128)S(1)}, f32[8,8,16,256]{3,2,1,0:T(8,128)S(1)}, u32[]{:S(2)}, u32[]{:S(2)}) collective-permute-start(f32[8,8,16,256]{3,2,1,0:T(8,128)S(1)} %copy-done.15), channel_id=1, source_target_pairs={{0,1},{1,0},{2,3},{3,2},{4,5},{5,4},{6,7},{7,6},{8,9},{9,8},{10,11... | collective-permute-start | bytes 3145736 | tf_op jit(solution)/shard_map/ppermute | solution.py:121
  419.9 55.5 %collective-permute-start.44 = (f32[8,8,16,256]{3,2,1,0:T(8,128)S(1)}, f32[8,8,16,256]{3,2,1,0:T(8,128)S(1)}, u32[]{:S(2)}, u32[]{:S(2)}) collective-permute-start(f32[8,8,16,256]{3,2,1,0:T(8,128)S(1)} %get-tuple-element.265), channel_id=1, source_target_pairs={{0,1},{1,0},{2,3},{3,2},{4,5},{5,4},{6,7},{7,6},{8,9},{9,8},{10,11... | collective-permute-start | bytes 3145736 | tf_op jit(solution)/shard_map/ppermute | solution.py:121
  475.7 56.3 %collective-permute-start.49 = (f32[8,8,16,256]{3,2,1,0:T(8,128)S(1)}, f32[8,8,16,256]{3,2,1,0:T(8,128)}, u32[]{:S(2)}, u32[]{:S(2)}) collective-permute-start(f32[8,8,16,256]{3,2,1,0:T(8,128)S(1)} %get-tuple-element.270), channel_id=1, source_target_pairs={{0,3},{1,2},{2,1},{3,0},{4,7},{5,6},{6,5},{7,4},{8,11},{9,10},{10,... | collective-permute-start | bytes 3145736 | tf_op jit(solution)/shard_map/ppermute | solution.py:121
  494.4 65.7 %collective-permute-start.56 = (f32[4,8,16,256]{3,2,1,0:T(8,128)S(1)}, f32[4,8,16,256]{3,2,1,0:T(8,128)S(1)}, u32[]{:S(2)}, u32[]{:S(2)}) collective-permute-start(f32[4,8,16,256]{3,2,1,0:T(8,128)S(1)} %pad_maximum_fusion.15), channel_id=1, source_target_pairs={{0,20},{4,16},{8,28},{12,24},{16,4},{20,0},{24,12},{28,8},{1,21},{... | collective-permute-start | bytes 1572872 | tf_op jit(solution)/shard_map/ppermute | solution.py:121
  528.9 64.0 %collective-permute-start.51 = (f32[4,8,16,256]{3,2,1,0:T(8,128)S(1)}, f32[4,8,16,256]{3,2,1,0:T(8,128)S(1)}, u32[]{:S(2)}, u32[]{:S(2)}) collective-permute-start(f32[4,8,16,256]{3,2,1,0:T(8,128)S(1)} %pad_maximum_fusion.9), channel_id=1, source_target_pairs={{0,12},{4,8},{8,20},{12,16},{16,28},{20,24},{24,4},{28,0},{1,13},{... | collective-permute-start | bytes 1572872 | tf_op jit(solution)/shard_map/ppermute | solution.py:121
  563.2 109.7 %collective-permute-start.59 = (f32[16,128,256]{2,1,0:T(8,128)}, f32[16,128,256]{2,1,0:T(8,128)S(1)}, u32[]{:S(2)}, u32[]{:S(2)}) collective-permute-start(f32[16,128,256]{2,1,0:T(8,128)} %get-tuple-element.289), channel_id=1, source_target_pairs={{0,2},{1,3},{2,0},{3,1},{4,6},{5,7},{6,4},{7,5},{8,10},{9,11},{10,... | collective-permute-start | bytes 6291464 | tf_op jit(solution)/shard_map/ppermute | solution.py:121
  604.4 90.4 %collective-permute-start.60 = (f32[16,128,256]{2,1,0:T(8,128)}, f32[16,128,256]{2,1,0:T(8,128)S(1)}, u32[]{:S(2)}, u32[]{:S(2)}) collective-permute-start(f32[16,128,256]{2,1,0:T(8,128)} %get-tuple-element.291), channel_id=1, source_target_pairs={{0,3},{1,2},{2,1},{3,0},{4,7},{5,6},{6,5},{7,4},{8,11},{9,10},{10,... | collective-permute-start | bytes 6291464 | tf_op jit(solution)/shard_map/ppermute | solution.py:121
  604.4 90.4 %collective-permute-start.58 = (f32[16,128,256]{2,1,0:T(8,128)}, f32[16,128,256]{2,1,0:T(8,128)S(1)}, u32[]{:S(2)}, u32[]{:S(2)}) collective-permute-start(f32[16,128,256]{2,1,0:T(8,128)} %get-tuple-element.287), channel_id=1, source_target_pairs={{0,1},{1,0},{2,3},{3,2},{4,5},{5,4},{6,7},{7,6},{8,9},{9,8},{10,11... | collective-permute-start | bytes 6291464 | tf_op jit(solution)/shard_map/ppermute | solution.py:121
  672.9 64.8 %collective-permute-start.69 = (f32[64,8,256]{2,1,0:T(8,128)}, f32[64,8,256]{2,1,0:T(8,128)}, u32[]{:S(2)}, u32[]{:S(2)}) collective-permute-start(f32[64,8,256]{2,1,0:T(8,128)} %get-tuple-element.311), channel_id=1, source_target_pairs={{0,24},{4,28},{8,0},{12,4},{16,8},{20,12},{24,16},{28,20},{1,25},{... | collective-permute-start | bytes 1572872 | tf_op jit(solution)/shard_map/ppermute | solution.py:121
  690.7 83.8 %collective-permute-start.73 = (f32[64,8,256]{2,1,0:T(8,128)}, f32[64,8,256]{2,1,0:T(8,128)}, u32[]{:S(2)}, u32[]{:S(2)}) collective-permute-start(f32[64,8,256]{2,1,0:T(8,128)} %get-tuple-element.318), channel_id=1, source_target_pairs={{0,20},{4,16},{8,28},{12,24},{16,4},{20,0},{24,12},{28,8},{1,21},{... | collective-permute-start | bytes 1572872 | tf_op jit(solution)/shard_map/ppermute | solution.py:121
  694.8 82.7 %collective-permute-start.72 = (f32[64,8,256]{2,1,0:T(8,128)}, f32[64,8,256]{2,1,0:T(8,128)}, u32[]{:S(2)}, u32[]{:S(2)}) collective-permute-start(f32[64,8,256]{2,1,0:T(8,128)} %get-tuple-element.316), channel_id=1, source_target_pairs={{0,12},{4,8},{8,20},{12,16},{16,28},{20,24},{24,4},{28,0},{1,13},{... | collective-permute-start | bytes 1572872 | tf_op jit(solution)/shard_map/ppermute | solution.py:121
  722.9 57.6 %collective-permute-start.71 = (f32[64,8,256]{2,1,0:T(8,128)}, f32[64,8,256]{2,1,0:T(8,128)}, u32[]{:S(2)}, u32[]{:S(2)}) collective-permute-start(f32[64,8,256]{2,1,0:T(8,128)} %get-tuple-element.314), channel_id=1, source_target_pairs={{0,28},{4,24},{8,4},{12,0},{16,12},{20,8},{24,20},{28,16},{1,29},{... | collective-permute-start | bytes 1572872 | tf_op jit(solution)/shard_map/ppermute | solution.py:121
  (99 other events, 4341.1 us)

commit v2 on v1

--- a/solution.py
+++ b/solution.py
@@ -103,12 +103,11 @@
     def work(self, function, s, value, *rest, back=True):
         out = function(s, after(value, *self.latest, *(self.back("px") if back else [])), *rest)
         self.latest = [jax.tree.leaves(out)[0]]
-        if back:
-            self.owe("work", self.latest[0])
+        self.owe("work", self.latest[0])
         return out
 
     def settle(self, depth):
-        self.due = [(0, array) for _, array in self.due] + [(0, array) for array in self.latest]
+        self.due = [(0, array) for _, array in self.due]
         self.depth["px"] = depth
 
     def permute(self, axis, block, pairs):
@@ -424,7 +423,7 @@
         first_ref[...] = value
         density_ref[...] = term_ref[...] + 0.05 * f_ref[...] * value
 
-    step = s.a // 2
+    step = s.a
     view = (s.a, s.nx, s.by, s.c)
     block = pl.BlockSpec((step, 1, s.yc, s.c), lambda i, source_ref: (i, source_ref[0], chunk, 0))
     touched = 6 * s.field_bytes // s.chunks // s.nx
@@ -531,7 +530,6 @@
     args = (0, potential, start_field, density, None, from_px)
     first, density = flow.work(finish_adjoint, s, a_out[0].rest(), *args, back=False)
     for chunk in range(1, s.chunks):
-        a_out[chunk].send(len(a_out[chunk].left) - 3)
         flow.settle(4)
         a_out[chunk].rest()
         for r in [0, *a_out[chunk].order]:

time: 788 us -> 785 us (level)
  starting transfers between devices: 131 us -> 118 us
    ppermute x74, starting transfers between devices: 131 us -> 118 us  [permute(): got = lax.ppermute(after(block, *pins), axis, pairs)]
  transfers between devices with their start and end apart: 74 -> 74, of which waited for: 44 -> 37; matrix products, arithmetic and copies ran while one was open for 1% -> 1% of each run, Pallas kernels for 18% -> 18%
where the time goes in v2:
time: 785 us; the launch traced here: 783 us
  waiting for transfers between devices  492 us (63%)
  Pallas kernels  151 us (19%)
  starting transfers between devices  118 us (15%)
  local copies, waits for them, and re-layouts  11.6 us (1%)
  other arithmetic  8.19 us (1%)
    ppermute x74, waiting for transfers between devices, permute(): got = lax.ppermute(after(block, *pins), axis, pairs)  492 us
    ppermute x74, starting transfers between devices, permute(): got = lax.ppermute(after(block, *pins), axis, pairs)  118 us
    pallas_call x8, Pallas kernels, finish_block(): pl.pallas_call(kernel, name='finish_block', grid_spec=pltpu.PrefetchScala...  25.7 us
    pallas_call x2, Pallas kernels, x_lines_adjoint(): call(kernel, 'x_lines_adjoint', (s.yc,), [table_spec()] * 3 + [whole_spec...  22.5 us
    pallas_call x2, Pallas kernels, x_lines_forward(): call(kernel, 'x_lines_forward', (s.yc,), [table_spec()] * 3 + [whole_spec...  20.7 us
    pallas_call x1, Pallas kernels, y_lines_turned(): call(kernel, 'y_lines_turned', (s.ax // ROWS,), [table_spec()] * 3 + [who...  17.9 us
    pallas_call x1, Pallas kernels, y_lines_unturned(): call(kernel, 'y_lines_unturned', (s.ax // ROWS,), [table_spec()] * 3 + [w...  16.8 us
  transfers between devices with their start and end apart: 74, of which 37 were waited for; matrix products, arithmetic and copies ran while one was open for 1% of the time, Pallas kernels for 18%

profile of v2, /device:TPU:12, one launch (start us, length us, event | category | flops | bytes accessed | tf_op | source)
XLA Modules:
  0.0 782.5 jit_solution(4320912285198266175)
XLA Ops:
  23.0 13.0 %collective-permute-done.rest_8_.rest_9_ = f32[64,8,256]{2,1,0:T(8,128)S(1)} collective-permute-done((f32[64,8,256]{2,1,0:T(8,128)}, f32[64,8,256]{2,1,0:T(8,128)S(1)}, u32[]{:S(2)}, u32[]{:S(2)}) %collective-permute-start) | collective-permute-done | bytes 524320 | tf_op jit(solution)/shard_map/ppermute | solution.py:120
  36.0 12.5 %collective-permute-start.4 = (f32[64,8,256]{2,1,0:T(8,128)}, f32[64,8,256]{2,1,0:T(8,128)}, u32[]{:S(2)}, u32[]{:S(2)}) collective-permute-start(f32[64,8,256]{2,1,0:T(8,128)} %get-tuple-element.181), channel_id=1, source_target_pairs={{0,12},{4,8},{8,20},{12,16},{16,28},{20,24},{24,4},{28,0},{1,13},{... | collective-permute-start | bytes 1572872 | tf_op jit(solution)/shard_map/ppermute | solution.py:120
  48.5 21.2 %collective-permute-done.1.rest_4_.rest_5_ = f32[64,8,256]{2,1,0:T(8,128)S(1)} collective-permute-done((f32[64,8,256]{2,1,0:T(8,128)}, f32[64,8,256]{2,1,0:T(8,128)S(1)}, u32[]{:S(2)}, u32[]{:S(2)}) %collective-permute-start.1) | collective-permute-done | bytes 524320 | tf_op jit(solution)/shard_map/ppermute | solution.py:120
  69.7 11.3 %collective-permute-done.2.rest_12_.rest_13_ = f32[64,8,256]{2,1,0:T(8,128)S(1)} collective-permute-done((f32[64,8,256]{2,1,0:T(8,128)}, f32[64,8,256]{2,1,0:T(8,128)S(1)}, u32[]{:S(2)}, u32[]{:S(2)}) %collective-permute-start.2) | collective-permute-done | bytes 524320 | tf_op jit(solution)/shard_map/ppermute | solution.py:120
  95.6 18.2 %collective-permute-done.4.rest_6_.rest_7_ = f32[64,8,256]{2,1,0:T(8,128)} collective-permute-done((f32[64,8,256]{2,1,0:T(8,128)}, f32[64,8,256]{2,1,0:T(8,128)}, u32[]{:S(2)}, u32[]{:S(2)}) %collective-permute-start.4) | collective-permute-done | bytes 524320 | tf_op jit(solution)/shard_map/ppermute | solution.py:120
  118.8 17.4 %collective-permute-done.7.rest_8_.rest_9_ = f32[64,8,256]{2,1,0:T(8,128)} collective-permute-done((f32[64,8,256]{2,1,0:T(8,128)S(1)}, f32[64,8,256]{2,1,0:T(8,128)}, u32[]{:S(2)}, u32[]{:S(2)}) %collective-permute-start.7) | collective-permute-done | bytes 524320 | tf_op jit(solution)/shard_map/ppermute | solution.py:120
  136.2 22.4 %collective-permute-done.13.rest_10_.rest_11_ = f32[64,8,256]{2,1,0:T(8,128)} collective-permute-done((f32[64,8,256]{2,1,0:T(8,128)S(1)}, f32[64,8,256]{2,1,0:T(8,128)}, u32[]{:S(2)}, u32[]{:S(2)}) %collective-permute-start.13) | collective-permute-done | bytes 524320 | tf_op jit(solution)/shard_map/ppermute | solution.py:120
  229.6 26.8 %collective-permute-done.19 = f32[4,8,16,256]{3,2,1,0:T(8,128)S(1)} collective-permute-done((f32[4,8,16,256]{3,2,1,0:T(8,128)}, f32[4,8,16,256]{3,2,1,0:T(8,128)S(1)}, u32[]{:S(2)}, u32[]{:S(2)}) %collective-permute-start.19) | collective-permute-done | bytes 524320 | tf_op jit(solution)/shard_map/ppermute | solution.py:120
  283.2 17.9 %y_lines_turned.1 = (f32[8,8,16,256]{3,2,1,0:T(8,128)}, f32[8,8,16,256]{3,2,1,0:T(8,128)}, f32[8,8,16,256]{3,2,1,0:T(8,128)}, f32[8,8,16,256]{3,2,1,0:T(8,128)},...) custom-call(s32[8]{0:T(128)} %fusion.13.to_ref.px_ref, ...), custom_call_target="tpu_custom_call" | custom-call | flops 6442450944 | bytes 16777216 | tf_op jit(solution)/shard_map/y_lines_turned/pallas_call | solution.py:347
  305.9 18.7 %collective-permute-done.24 = f32[4,8,16,256]{3,2,1,0:T(8,128)S(1)} collective-permute-done((f32[4,8,16,256]{3,2,1,0:T(8,128)}, f32[4,8,16,256]{3,2,1,0:T(8,128)S(1)}, u32[]{:S(2)}, u32[]{:S(2)}) %collective-permute-start.24) | collective-permute-done | bytes 524320 | tf_op jit(solution)/shard_map/ppermute | solution.py:120
  358.7 21.7 %collective-permute-done.34 = f32[4,8,16,256]{3,2,1,0:T(8,128)S(1)} collective-permute-done((f32[4,8,16,256]{3,2,1,0:T(8,128)S(1)}, f32[4,8,16,256]{3,2,1,0:T(8,128)S(1)}, u32[]{:S(2)}, u32[]{:S(2)}) %collective-permute-start.34) | collective-permute-done | bytes 524320 | tf_op jit(solution)/shard_map/ppermute | solution.py:120
  395.6 22.8 %collective-permute-done.38.rest_4_ = f32[4,8,16,256]{3,2,1,0:T(8,128)S(1)} collective-permute-done((f32[4,8,16,256]{3,2,1,0:T(8,128)S(1)}, f32[4,8,16,256]{3,2,1,0:T(8,128)S(1)}, u32[]{:S(2)}, u32[]{:S(2)}) %collective-permute-start.38) | collective-permute-done | bytes 524320 | tf_op jit(solution)/shard_map/ppermute | solution.py:120
  448.4 26.7 %collective-permute-done.37.rest_5_ = f32[4,8,16,256]{3,2,1,0:T(8,128)S(1)} collective-permute-done((f32[4,8,16,256]{3,2,1,0:T(8,128)S(1)}, f32[4,8,16,256]{3,2,1,0:T(8,128)S(1)}, u32[]{:S(2)}, u32[]{:S(2)}) %collective-permute-start.37) | collective-permute-done | bytes 524320 | tf_op jit(solution)/shard_map/ppermute | solution.py:120
  493.2 39.9 %collective-permute-done.50.rest_4_ = f32[4,8,16,256]{3,2,1,0:T(8,128)S(1)} collective-permute-done((f32[4,8,16,256]{3,2,1,0:T(8,128)S(1)}, f32[4,8,16,256]{3,2,1,0:T(8,128)S(1)}, u32[]{:S(2)}, u32[]{:S(2)}) %collective-permute-start.50) | collective-permute-done | bytes 524320 | tf_op jit(solution)/shard_map/ppermute | solution.py:120
  541.1 16.8 %y_lines_unturned.1 = (f32[16,128,256]{2,1,0:T(8,128)}, f32[16,128,256]{2,1,0:T(8,128)}, f32[16,128,256]{2,1,0:T(8,128)}, f32[16,128,256]{2,1,0:T(8,128)}) custom-call(s32[8]{0:T(128)} %fusion.9.from_ref.px_ref, s32[4]{0:T(128)} %fusion.7.from_ref.part_ref, s32[4]{0:T(128)} %fusion.11.to_ref.part_ref, bf16[512,512]{1,0:T(8,128)(2,1)} %get-tuple-element.406.high_ref, ...), custom_call_target="tpu_custom_call" | custom-call | flops 6442450944 | bytes 16777216 | tf_op jit(solution)/shard_map/y_lines_unturned/pallas_call | solution.py:309
  557.9 11.3 %x_lines_adjoint.2 = (f32[64,8,256]{2,1,0:T(8,128)}, f32[64,8,256]{2,1,0:T(8,128)}, f32[64,8,256]{2,1,0:T(8,128)}, f32[64,8,256]{2,1,0:T(8,128)}, f32[64,8,256]{...) custom-call(s32[8]{0:T(128)} %fusion.9.from_ref.px_ref, ...), custom_call_target="tpu_custom_call" | custom-call | flops 3221225472 | bytes 8388608 | tf_op jit(solution)/shard_map/x_lines_adjoint/pallas_call | solution.py:267
  569.2 19.4 %collective-permute-done.51.rest_3_ = f32[4,8,16,256]{3,2,1,0:T(8,128)} collective-permute-done((f32[4,8,16,256]{3,2,1,0:T(8,128)S(1)}, f32[4,8,16,256]{3,2,1,0:T(8,128)}, u32[]{:S(2)}, u32[]{:S(2)}) %collective-permute-start.51) | collective-permute-done | bytes 524320 | tf_op jit(solution)/shard_map/ppermute | solution.py:120
  588.8 16.7 %collective-permute-done.57.rest_4_ = f32[64,8,256]{2,1,0:T(8,128)S(1)} collective-permute-done((f32[64,8,256]{2,1,0:T(8,128)}, f32[64,8,256]{2,1,0:T(8,128)S(1)}, u32[]{:S(2)}, u32[]{:S(2)}) %collective-permute-start.57) | collective-permute-done | bytes 524320 | tf_op jit(solution)/shard_map/ppermute | solution.py:120
  612.3 15.0 %collective-permute-done.64.rest_5_ = f32[64,8,256]{2,1,0:T(8,128)S(1)} collective-permute-done((f32[64,8,256]{2,1,0:T(8,128)}, f32[64,8,256]{2,1,0:T(8,128)S(1)}, u32[]{:S(2)}, u32[]{:S(2)}) %collective-permute-start.64) | collective-permute-done | bytes 524320 | tf_op jit(solution)/shard_map/ppermute | solution.py:120
  627.3 11.3 %x_lines_adjoint.3 = (f32[64,8,256]{2,1,0:T(8,128)}, f32[64,8,256]{2,1,0:T(8,128)}, f32[64,8,256]{2,1,0:T(8,128)}, f32[64,8,256]{2,1,0:T(8,128)}, f32[64,8,256]{...) custom-call(s32[8]{0:T(128)} %fusion.9.from_ref.px_ref, ...), custom_call_target="tpu_custom_call" | custom-call | flops 3221225472 | bytes 8388608 | tf_op jit(solution)/shard_map/x_lines_adjoint/pallas_call | solution.py:267
  648.2 20.5 %collective-permute-done.65.got_ref = f32[64,8,256]{2,1,0:T(8,128)S(1)} collective-permute-done((f32[64,8,256]{2,1,0:T(8,128)}, f32[64,8,256]{2,1,0:T(8,128)S(1)}, u32[]{:S(2)}, u32[]{:S(2)}) %collective-permute-start.65) | collective-permute-done | bytes 524320 | tf_op jit(solution)/shard_map/ppermute | solution.py:120
  668.6 15.5 %collective-permute-start.68 = (f32[64,8,256]{2,1,0:T(8,128)}, f32[64,8,256]{2,1,0:T(8,128)S(1)}, u32[]{:S(2)}, u32[]{:S(2)}) collective-permute-start(f32[64,8,256]{2,1,0:T(8,128)} %get-tuple-element.310), channel_id=1, source_target_pairs={{0,28},{4,24},{8,4},{12,0},{16,12},{20,8},{24,20},{28,16},{1,29},{... | collective-permute-start | bytes 1572872 | tf_op jit(solution)/shard_map/ppermute | solution.py:120
  711.6 14.0 %finish_forward.1 = (f32[4,16,128,256]{3,2,1,0:T(8,128)}, f32[4,16,128,256]{3,2,1,0:T(8,128)}) custom-call(s32[4]{0:T(128)} %fusion.7.from_ref.part_ref, f32[4,16,128,256]{3,2,1,0:T(8,128)} %bitcast.19, f32[4,16,128,256]{3,2,1,0:T(8,128)} %bitcast.44, f32[16,128,256]{2,1,0:T(8,128)} %get-tuple-element.285.rest_0_, f32[16,128,256]{2,1,0:T(8,128)} %copy-done.3, ...), custom_call_target="tpu_custom_call" | custom-call | flops 8388608 | bytes 41943040 | tf_op jit(solution)/shard_map/finish_forward/pallas_call | solution.py:379
  757.0 13.5 %collective-permute-done.72.got_ref = f32[64,8,256]{2,1,0:T(8,128)S(1)} collective-permute-done((f32[64,8,256]{2,1,0:T(8,128)}, f32[64,8,256]{2,1,0:T(8,128)S(1)}, u32[]{:S(2)}, u32[]{:S(2)}) %collective-permute-start.72) | collective-permute-done | bytes 524320 | tf_op jit(solution)/shard_map/ppermute | solution.py:120
  (310 shorter events, 336.4 us)
Async XLA Ops:
  12.4 57.2 %collective-permute-start.1 = (f32[64,8,256]{2,1,0:T(8,128)}, f32[64,8,256]{2,1,0:T(8,128)S(1)}, u32[]{:S(2)}, u32[]{:S(2)}) collective-permute-start(f32[64,8,256]{2,1,0:T(8,128)} %get-tuple-element.175), channel_id=1, source_target_pairs={{0,8},{4,12},{8,16},{12,20},{16,24},{20,28},{24,0},{28,4},{1,9},{5... | collective-permute-start | bytes 1572872 | tf_op jit(solution)/shard_map/ppermute | solution.py:120
  12.4 68.5 %collective-permute-start.2 = (f32[64,8,256]{2,1,0:T(8,128)}, f32[64,8,256]{2,1,0:T(8,128)S(1)}, u32[]{:S(2)}, u32[]{:S(2)}) collective-permute-start(f32[64,8,256]{2,1,0:T(8,128)} %get-tuple-element.178), channel_id=1, source_target_pairs={{0,24},{4,28},{8,0},{12,4},{16,8},{20,12},{24,16},{28,20},{1,25},{... | collective-permute-start | bytes 1572872 | tf_op jit(solution)/shard_map/ppermute | solution.py:120
  14.5 80.3 %collective-permute-start.3 = (f32[64,8,256]{2,1,0:T(8,128)}, f32[64,8,256]{2,1,0:T(8,128)}, u32[]{:S(2)}, u32[]{:S(2)}) collective-permute-start(f32[64,8,256]{2,1,0:T(8,128)} %get-tuple-element.179), channel_id=1, source_target_pairs={{0,20},{4,16},{8,28},{12,24},{16,4},{20,0},{24,12},{28,8},{1,21},{... | collective-permute-start | bytes 1572872 | tf_op jit(solution)/shard_map/ppermute | solution.py:120
  36.0 77.8 %collective-permute-start.4 = (f32[64,8,256]{2,1,0:T(8,128)}, f32[64,8,256]{2,1,0:T(8,128)}, u32[]{:S(2)}, u32[]{:S(2)}) collective-permute-start(f32[64,8,256]{2,1,0:T(8,128)} %get-tuple-element.181), channel_id=1, source_target_pairs={{0,12},{4,8},{8,20},{12,16},{16,28},{20,24},{24,4},{28,0},{1,13},{... | collective-permute-start | bytes 1572872 | tf_op jit(solution)/shard_map/ppermute | solution.py:120
  94.2 119.8 %collective-permute-start.16 = (f32[16,128,256]{2,1,0:T(8,128)}, f32[16,128,256]{2,1,0:T(8,128)}, u32[]{:S(2)}, u32[]{:S(2)}) collective-permute-start(f32[16,128,256]{2,1,0:T(8,128)} %get-tuple-element.210), channel_id=1, source_target_pairs={{0,2},{1,3},{2,0},{3,1},{4,6},{5,7},{6,4},{7,5},{8,10},{9,11},{10,... | collective-permute-start | bytes 6291464 | tf_op jit(solution)/shard_map/ppermute | solution.py:120
  115.8 54.1 %collective-permute-start.9 = (f32[64,8,256]{2,1,0:T(8,128)}, f32[64,8,256]{2,1,0:T(8,128)S(1)}, u32[]{:S(2)}, u32[]{:S(2)}) collective-permute-start(f32[64,8,256]{2,1,0:T(8,128)} %get-tuple-element.194), channel_id=1, source_target_pairs={{0,8},{4,12},{8,16},{12,20},{16,24},{20,28},{24,0},{28,4},{1,9},{5... | collective-permute-start | bytes 1572872 | tf_op jit(solution)/shard_map/ppermute | solution.py:120
  117.3 63.7 %collective-permute-start.11 = (f32[64,8,256]{2,1,0:T(8,128)}, f32[64,8,256]{2,1,0:T(8,128)S(1)}, u32[]{:S(2)}, u32[]{:S(2)}) collective-permute-start(f32[64,8,256]{2,1,0:T(8,128)} %get-tuple-element.198), channel_id=1, source_target_pairs={{0,24},{4,28},{8,0},{12,4},{16,8},{20,12},{24,16},{28,20},{1,25},{... | collective-permute-start | bytes 1572872 | tf_op jit(solution)/shard_map/ppermute | solution.py:120
  136.2 133.9 %collective-permute-start.17 = (f32[16,128,256]{2,1,0:T(8,128)}, f32[16,128,256]{2,1,0:T(8,128)}, u32[]{:S(2)}, u32[]{:S(2)}) collective-permute-start(f32[16,128,256]{2,1,0:T(8,128)} %get-tuple-element.212), channel_id=1, source_target_pairs={{0,3},{1,2},{2,1},{3,0},{4,7},{5,6},{6,5},{7,4},{8,11},{9,10},{10,... | collective-permute-start | bytes 6291464 | tf_op jit(solution)/shard_map/ppermute | solution.py:120
  158.7 124.5 %collective-permute-start.15 = (f32[16,128,256]{2,1,0:T(8,128)}, f32[16,128,256]{2,1,0:T(8,128)}, u32[]{:S(2)}, u32[]{:S(2)}) collective-permute-start(f32[16,128,256]{2,1,0:T(8,128)} %get-tuple-element.208), channel_id=1, source_target_pairs={{0,1},{1,0},{2,3},{3,2},{4,5},{5,4},{6,7},{7,6},{8,9},{9,8},{10,11... | collective-permute-start | bytes 6291464 | tf_op jit(solution)/shard_map/ppermute | solution.py:120
  214.0 56.0 %collective-permute-start.21 = (f32[4,8,16,256]{3,2,1,0:T(8,128)}, f32[4,8,16,256]{3,2,1,0:T(8,128)S(1)}, u32[]{:S(2)}, u32[]{:S(2)}) collective-permute-start(f32[4,8,16,256]{3,2,1,0:T(8,128)} %get-tuple-element.222), channel_id=1, source_target_pairs={{0,24},{4,28},{8,0},{12,4},{16,8},{20,12},{24,16},{28,20},{1,25},{... | collective-permute-start | bytes 1572872 | tf_op jit(solution)/shard_map/ppermute | solution.py:120
  222.8 56.1 %collective-permute-start.23 = (f32[4,8,16,256]{3,2,1,0:T(8,128)}, f32[4,8,16,256]{3,2,1,0:T(8,128)S(1)}, u32[]{:S(2)}, u32[]{:S(2)}) collective-permute-start(f32[4,8,16,256]{3,2,1,0:T(8,128)} %get-tuple-element.226), channel_id=1, source_target_pairs={{0,20},{4,16},{8,28},{12,24},{16,4},{20,0},{24,12},{28,8},{1,21},{... | collective-permute-start | bytes 1572872 | tf_op jit(solution)/shard_map/ppermute | solution.py:120
  347.5 71.0 %collective-permute-start.31 = (f32[8,8,16,256]{3,2,1,0:T(8,128)}, f32[8,8,16,256]{3,2,1,0:T(8,128)S(1)}, u32[]{:S(2)}, u32[]{:S(2)}) collective-permute-start(f32[8,8,16,256]{3,2,1,0:T(8,128)} %get-tuple-element.245), channel_id=1, source_target_pairs={{0,2},{1,3},{2,0},{3,1},{4,6},{5,7},{6,4},{7,5},{8,10},{9,11},{10,... | collective-permute-start | bytes 3145736 | tf_op jit(solution)/shard_map/ppermute | solution.py:120
  350.0 72.7 %collective-permute-start.32 = (f32[8,8,16,256]{3,2,1,0:T(8,128)}, f32[8,8,16,256]{3,2,1,0:T(8,128)S(1)}, u32[]{:S(2)}, u32[]{:S(2)}) collective-permute-start(f32[8,8,16,256]{3,2,1,0:T(8,128)} %get-tuple-element.247), channel_id=1, source_target_pairs={{0,3},{1,2},{2,1},{3,0},{4,7},{5,6},{6,5},{7,4},{8,11},{9,10},{10,... | collective-permute-start | bytes 3145736 | tf_op jit(solution)/shard_map/ppermute | solution.py:120
  358.6 64.2 %collective-permute-start.30 = (f32[8,8,16,256]{3,2,1,0:T(8,128)S(1)}, f32[8,8,16,256]{3,2,1,0:T(8,128)S(1)}, u32[]{:S(2)}, u32[]{:S(2)}) collective-permute-start(f32[8,8,16,256]{3,2,1,0:T(8,128)S(1)} %copy-done.22), channel_id=1, source_target_pairs={{0,1},{1,0},{2,3},{3,2},{4,5},{5,4},{6,7},{7,6},{8,9},{9,8},{10,11... | collective-permute-start | bytes 3145736 | tf_op jit(solution)/shard_map/ppermute | solution.py:120
  423.8 52.3 %collective-permute-start.44 = (f32[8,8,16,256]{3,2,1,0:T(8,128)S(1)}, f32[8,8,16,256]{3,2,1,0:T(8,128)S(1)}, u32[]{:S(2)}, u32[]{:S(2)}) collective-permute-start(f32[8,8,16,256]{3,2,1,0:T(8,128)S(1)} %get-tuple-element.265), channel_id=1, source_target_pairs={{0,1},{1,0},{2,3},{3,2},{4,5},{5,4},{6,7},{7,6},{8,9},{9,8},{10,11... | collective-permute-start | bytes 3145736 | tf_op jit(solution)/shard_map/ppermute | solution.py:120
  423.8 52.2 %collective-permute-start.45 = (f32[8,8,16,256]{3,2,1,0:T(8,128)S(1)}, f32[8,8,16,256]{3,2,1,0:T(8,128)S(1)}, u32[]{:S(2)}, u32[]{:S(2)}) collective-permute-start(f32[8,8,16,256]{3,2,1,0:T(8,128)S(1)} %get-tuple-element.266), channel_id=1, source_target_pairs={{0,2},{1,3},{2,0},{3,1},{4,6},{5,7},{6,4},{7,5},{8,10},{9,11},{10,... | collective-permute-start | bytes 3145736 | tf_op jit(solution)/shard_map/ppermute | solution.py:120
  424.2 51.8 %collective-permute-start.46 = (f32[8,8,16,256]{3,2,1,0:T(8,128)S(1)}, f32[8,8,16,256]{3,2,1,0:T(8,128)S(1)}, u32[]{:S(2)}, u32[]{:S(2)}) collective-permute-start(f32[8,8,16,256]{3,2,1,0:T(8,128)S(1)} %get-tuple-element.267), channel_id=1, source_target_pairs={{0,3},{1,2},{2,1},{3,0},{4,7},{5,6},{6,5},{7,4},{8,11},{9,10},{10,... | collective-permute-start | bytes 3145736 | tf_op jit(solution)/shard_map/ppermute | solution.py:120
  476.1 60.9 %collective-permute-start.47 = (f32[8,8,16,256]{3,2,1,0:T(8,128)S(1)}, f32[8,8,16,256]{3,2,1,0:T(8,128)S(1)}, u32[]{:S(2)}, u32[]{:S(2)}) collective-permute-start(f32[8,8,16,256]{3,2,1,0:T(8,128)S(1)} %get-tuple-element.268), channel_id=1, source_target_pairs={{0,1},{1,0},{2,3},{3,2},{4,5},{5,4},{6,7},{7,6},{8,9},{9,8},{10,11... | collective-permute-start | bytes 3145736 | tf_op jit(solution)/shard_map/ppermute | solution.py:120
  476.2 63.8 %collective-permute-start.48 = (f32[8,8,16,256]{3,2,1,0:T(8,128)S(1)}, f32[8,8,16,256]{3,2,1,0:T(8,128)S(1)}, u32[]{:S(2)}, u32[]{:S(2)}) collective-permute-start(f32[8,8,16,256]{3,2,1,0:T(8,128)S(1)} %get-tuple-element.269), channel_id=1, source_target_pairs={{0,2},{1,3},{2,0},{3,1},{4,6},{5,7},{6,4},{7,5},{8,10},{9,11},{10,... | collective-permute-start | bytes 3145736 | tf_op jit(solution)/shard_map/ppermute | solution.py:120
  479.4 61.7 %collective-permute-start.49 = (f32[8,8,16,256]{3,2,1,0:T(8,128)S(1)}, f32[8,8,16,256]{3,2,1,0:T(8,128)}, u32[]{:S(2)}, u32[]{:S(2)}) collective-permute-start(f32[8,8,16,256]{3,2,1,0:T(8,128)S(1)} %get-tuple-element.270), channel_id=1, source_target_pairs={{0,3},{1,2},{2,1},{3,0},{4,7},{5,6},{6,5},{7,4},{8,11},{9,10},{10,... | collective-permute-start | bytes 3145736 | tf_op jit(solution)/shard_map/ppermute | solution.py:120
  537.1 51.5 %collective-permute-start.51 = (f32[4,8,16,256]{3,2,1,0:T(8,128)S(1)}, f32[4,8,16,256]{3,2,1,0:T(8,128)}, u32[]{:S(2)}, u32[]{:S(2)}) collective-permute-start(f32[4,8,16,256]{3,2,1,0:T(8,128)S(1)} %pad_maximum_fusion.9), channel_id=1, source_target_pairs={{0,12},{4,8},{8,20},{12,16},{16,28},{20,24},{24,4},{28,0},{1,13},{... | collective-permute-start | bytes 1572872 | tf_op jit(solution)/shard_map/ppermute | solution.py:120
  588.6 120.2 %collective-permute-start.60 = (f32[16,128,256]{2,1,0:T(8,128)}, f32[16,128,256]{2,1,0:T(8,128)S(1)}, u32[]{:S(2)}, u32[]{:S(2)}) collective-permute-start(f32[16,128,256]{2,1,0:T(8,128)} %get-tuple-element.291), channel_id=1, source_target_pairs={{0,3},{1,2},{2,1},{3,0},{4,7},{5,6},{6,5},{7,4},{8,11},{9,10},{10,... | collective-permute-start | bytes 6291464 | tf_op jit(solution)/shard_map/ppermute | solution.py:120
  588.7 120.1 %collective-permute-start.59 = (f32[16,128,256]{2,1,0:T(8,128)}, f32[16,128,256]{2,1,0:T(8,128)S(1)}, u32[]{:S(2)}, u32[]{:S(2)}) collective-permute-start(f32[16,128,256]{2,1,0:T(8,128)} %get-tuple-element.289), channel_id=1, source_target_pairs={{0,2},{1,3},{2,0},{3,1},{4,6},{5,7},{6,4},{7,5},{8,10},{9,11},{10,... | collective-permute-start | bytes 6291464 | tf_op jit(solution)/shard_map/ppermute | solution.py:120
  605.6 103.3 %collective-permute-start.58 = (f32[16,128,256]{2,1,0:T(8,128)}, f32[16,128,256]{2,1,0:T(8,128)S(1)}, u32[]{:S(2)}, u32[]{:S(2)}) collective-permute-start(f32[16,128,256]{2,1,0:T(8,128)} %get-tuple-element.287), channel_id=1, source_target_pairs={{0,1},{1,0},{2,3},{3,2},{4,5},{5,4},{6,7},{7,6},{8,9},{9,8},{10,11... | collective-permute-start | bytes 6291464 | tf_op jit(solution)/shard_map/ppermute | solution.py:120
  (108 other events, 3855.1 us)
